TPU v7x, 128 devices: a whole 4x4x4 slice. The times are simulated.
128 devices in a mesh: dp: 8 (over z, x_hi), ctx: 16 (over y, x_lo, core).
Axes of the slice: x: 4 (x_hi: 2, x_lo: 2; x = x_hi * 2 + x_lo), y: 4, z: 4, core: 2. Of those that a mesh axis runs over, the one named last changes fastest.
Arguments:
- queries: bfloat16 [16384, 4096], P(('dp', 'ctx')), may hold values from -6 to 6
- keys: bfloat16 [16384, 4096], P(('dp', 'ctx')), may hold values from -6 to 6
- values: bfloat16 [16384, 4096], P(('dp', 'ctx')), may hold values from -6 to 6
- grad_out: bfloat16 [16384, 4096], P(('dp', 'ctx')), may hold values from -6 to 6
- filter_param: float32 [16384, 4096], P(None, ('dp', 'ctx')), may hold values from -6 to 6
Outputs:
- query_grad: bfloat16 [16384, 4096], P(('dp', 'ctx'))
- key_grad: bfloat16 [16384, 4096], P(('dp', 'ctx'))
- value_grad: bfloat16 [16384, 4096], P(('dp', 'ctx'))
- filter_grad: float32 [16384, 4096], P(None, ('dp', 'ctx'))
All inputs are finite; a program needn't handle non-finite values.
Results may differ from a plain program's by a relative error of at most 0.022.
Values may be sent and summed in bfloat16 or wider, within the bound.
A program may use at most 320 MiB of HBM per device.

v0:
```python
import math

import jax
import jax.numpy as jnp
from jax import lax
from jax.sharding import PartitionSpec as P


def make_tables(outer, inner):
    total = outer * inner
    first = jnp.arange(outer, dtype=jnp.int32)
    second = jnp.arange(inner, dtype=jnp.int32)
    phase_one = (first[:, None] * first[None, :] % outer).astype(jnp.float32) * (
        2.0 * math.pi / outer
    )
    phase_two = (second[:, None] * second[None, :] % inner).astype(jnp.float32) * (
        2.0 * math.pi / inner
    )
    phase_twist = (first[:, None] * second[None, :] % total).astype(jnp.float32) * (
        2.0 * math.pi / total
    )
    return (
        jnp.cos(phase_one),
        jnp.sin(phase_one),
        jnp.cos(phase_two),
        jnp.sin(phase_two),
        jnp.cos(phase_twist),
        jnp.sin(phase_twist),
    )


def split_parts(array):
    upper = array.astype(jnp.bfloat16)
    lower = (array - upper.astype(jnp.float32)).astype(jnp.bfloat16)
    return (upper, lower)


def mixed(form, matrix, data):
    upper, lower = split_parts(matrix)
    if data.dtype == jnp.bfloat16:
        return jnp.einsum(form, upper, data, preferred_element_type=jnp.float32) + jnp.einsum(
            form, lower, data, preferred_element_type=jnp.float32
        )
    data_upper, data_lower = split_parts(data)
    return (
        jnp.einsum(form, upper, data_upper, preferred_element_type=jnp.float32)
        + jnp.einsum(form, upper, data_lower, preferred_element_type=jnp.float32)
        + jnp.einsum(form, lower, data_upper, preferred_element_type=jnp.float32)
    )


def along_inner(matrix, array):
    return mixed("gb,kbw->kgw", matrix, array)


def forward_transform(signal, tables):
    first_cos, first_sin, second_cos, second_sin, twist_cos, twist_sin = tables
    outer = first_cos.shape[0]
    half = outer // 2
    inner = second_cos.shape[0]
    width = signal.shape[1]
    flat = signal.reshape(half, inner, width)
    real_a = mixed("ka,abw->kbw", first_cos[:, :half], flat)
    imag_a = -mixed("ka,abw->kbw", first_sin[:, :half], flat)
    real_b = real_a * twist_cos[:, :, None] + imag_a * twist_sin[:, :, None]
    imag_b = imag_a * twist_cos[:, :, None] - real_a * twist_sin[:, :, None]
    real_x = along_inner(second_cos, real_b) + along_inner(second_sin, imag_b)
    imag_x = along_inner(second_cos, imag_b) - along_inner(second_sin, real_b)
    return (real_x, imag_x)


def inverse_transform(spectrum, tables):
    first_cos, first_sin, second_cos, second_sin, twist_cos, twist_sin = tables
    real_x, imag_x = spectrum
    outer, inner, width = real_x.shape
    half = outer // 2
    real_b = along_inner(second_cos, real_x) - along_inner(second_sin, imag_x)
    imag_b = along_inner(second_cos, imag_x) + along_inner(second_sin, real_x)
    real_c = real_b * twist_cos[:, :, None] - imag_b * twist_sin[:, :, None]
    imag_c = imag_b * twist_cos[:, :, None] + real_b * twist_sin[:, :, None]
    signal = mixed("ak,kbw->abw", first_cos[:half], real_c)
    signal = signal - mixed("ak,kbw->abw", first_sin[:half], imag_c)
    return (signal / (outer * inner)).reshape(half * inner, width)


def product(left, right):
    return (left[0] * right[0] - left[1] * right[1], left[0] * right[1] + left[1] * right[0])


def conj_product(left, right):
    return (left[0] * right[0] + left[1] * right[1], left[0] * right[1] - left[1] * right[0])


def local(queries, keys, values, grad_out, filter_param):
    gated = (keys.astype(jnp.float32) * values.astype(jnp.float32)).astype(jnp.bfloat16)
    gated_grad = (grad_out.astype(jnp.float32) * queries.astype(jnp.float32)).astype(jnp.bfloat16)
    tokens, width = gated.shape
    groups_dp = lax.axis_size("dp")
    groups_ctx = lax.axis_size("ctx")
    length = tokens * groups_dp * groups_ctx
    scale = 1.0 / math.sqrt(length)
    tables = make_tables(2 * length // 128, 128)
    taps = filter_param * scale
    moved, moved_grad = (
        lax.all_to_all(gated, ("dp", "ctx"), split_axis=1, concat_axis=0, tiled=True),
        lax.all_to_all(gated_grad, ("dp", "ctx"), split_axis=1, concat_axis=0, tiled=True),
    )
    spectrum_taps = forward_transform(taps, tables)
    spectrum_gated = forward_transform(moved, tables)
    spectrum_grad = forward_transform(moved_grad, tables)
    conv_all = inverse_transform(product(spectrum_taps, spectrum_gated), tables).astype(
        jnp.bfloat16
    )
    back_all = inverse_transform(conj_product(spectrum_taps, spectrum_grad), tables).astype(
        jnp.bfloat16
    )
    filter_grad = inverse_transform(conj_product(spectrum_gated, spectrum_grad), tables) * scale
    conv_out, gated_back = (
        lax.all_to_all(conv_all, ("dp", "ctx"), split_axis=0, concat_axis=1, tiled=True),
        lax.all_to_all(back_all, ("dp", "ctx"), split_axis=0, concat_axis=1, tiled=True),
    )
    query_grad = (grad_out.astype(jnp.float32) * conv_out.astype(jnp.float32)).astype(jnp.bfloat16)
    key_grad = (gated_back.astype(jnp.float32) * values.astype(jnp.float32)).astype(jnp.bfloat16)
    value_grad = (gated_back.astype(jnp.float32) * keys.astype(jnp.float32)).astype(jnp.bfloat16)
    return (query_grad, key_grad, value_grad, filter_grad)


def solution(mesh):
    in_specs = (
        P(("dp", "ctx"), None),
        P(("dp", "ctx"), None),
        P(("dp", "ctx"), None),
        P(("dp", "ctx"), None),
        P(None, ("dp", "ctx")),
    )
    out_specs = (
        P(("dp", "ctx"), None),
        P(("dp", "ctx"), None),
        P(("dp", "ctx"), None),
        P(None, ("dp", "ctx")),
    )
    return jax.shard_map(local, mesh=mesh, in_specs=in_specs, out_specs=out_specs, check_vma=False)
```

profile of v0, /device:TPU:1, one launch (start us, length us, event | category | flops | bytes accessed | tf_op | source)
XLA Modules:
  0.0 496.4 jit_solution(3636040196499016039)
XLA Ops:
  5.6 11.5 %all-to-all-start = ((bf16[128,128,32]{0,2,1:T(8,128)(2,1)}), bf16[128,128,32]{0,2,1:T(8,128)(2,1)S(1)}, u32[]{:S(2)}, u32[]{:S(2)}) async-start(bf16[128,128,32]{0,2,1:T(8,128)(2,1)} %bitcast.9), calls=%async_computation | async-start | bytes 2097152 | tf_op jit(solution)/shard_map/all_to_all | solution.py:105
  36.4 9.8 %all-to-all-start.2 = ((bf16[128,128,32]{0,2,1:T(8,128)(2,1)}), bf16[128,128,32]{0,2,1:T(8,128)(2,1)S(1)}, u32[]{:S(2)}, u32[]{:S(2)}) async-start(bf16[128,128,32]{0,2,1:T(8,128)(2,1)} %bitcast.656), calls=%async_computation.2 | async-start | bytes 2097152 | tf_op jit(solution)/shard_map/all_to_all | solution.py:106
  53.9 11.6 %all-to-all-done.2 = bf16[128,128,32]{0,2,1:T(8,128)(2,1)S(1)} async-done(((bf16[128,128,32]{0,2,1:T(8,128)(2,1)}), bf16[128,128,32]{0,2,1:T(8,128)(2,1)S(1)}, u32[]{:S(2)}, u32[]{:S(2)}) %all-to-all-start.2) | async-done | bytes 1048608 | tf_op jit(solution)/shard_map/all_to_all | solution.py:106
  78.4 16.0 %subtract_convert_fusion.1 = (bf16[256,128,32]{1,0,2:T(8,128)(2,1)}, bf16[256,128,32]{1,0,2:T(8,128)(2,1)}, bf16[256,128,32]{1,0,2:T(8,128)(2,1)}, bf16[256,128,...) fusion(f32[256,128]{1,0:T(8,128)S(1)} %get-tuple-element.71, ...), kind=kOutput, calls=%fused_computation.52 | convolution fusion | flops 314572800 | bytes 51707904 | tf_op jit(solution)/shard_map/ka,abw->kbw/dot_general | solution.py:41
  94.4 4.7 fusion.251
  180.8 11.1 %add_subtract_fusion.2 = f32[256,32,128]{2,0,1:T(8,128)} fusion(f32[256,32,128]{2,0,1:T(8,128)} %fusion.138, f32[256,32,128]{2,0,1:T(8,128)} %fusion.136, f32[256,32,128]{2,0,1:T(8,128)} %fusion.251, f32[256,32,128]{2,0,1:T(8,128)} %fusion.186, f32[256,32,128]{2,0,1:T(8,128)} %fusion.184, bf16[256,128,32]{1,0,2:T(8,128)(2,1)S(1)} %copy-done.15), kind=kOutput, calls=%fused_computation.48 | convolution fusion | flops 273973248 | bytes 27262976 | tf_op jit(solution)/shard_map/gb,kbw->kgw/dot_general | solution.py:48
  191.9 10.9 %add_add_fusion.4 = f32[256,32,128]{2,0,1:T(8,128)} fusion(f32[256,32,128]{2,0,1:T(8,128)} %fusion.162, f32[256,32,128]{2,0,1:T(8,128)} %fusion.160, f32[256,32,128]{2,0,1:T(8,128)} %fusion.263, f32[256,32,128]{2,0,1:T(8,128)} %fusion.210, f32[256,32,128]{2,0,1:T(8,128)} %fusion.208, bf16[256,128,32]{1,0,2:T(8,128)(2,1)S(1)} %copy-done.14), kind=kOutput, calls=%fused_computation.63 | convolution fusion | flops 273973248 | bytes 27262976 | tf_op jit(solution)/shard_map/gb,kbw->kgw/dot_general | solution.py:48
  202.8 8.7 %add_add_fusion.2 = f32[256,32,128]{2,0,1:T(8,128)} fusion(f32[256,32,128]{2,0,1:T(8,128)S(1)} %fusion.142, f32[256,32,128]{2,0,1:T(8,128)S(1)} %copy-done.33, f32[256,32,128]{2,0,1:T(8,128)} %fusion.253, f32[256,32,128]{2,0,1:T(8,128)} %fusion.190, f32[256,32,128]{2,0,1:T(8,128)} %fusion.188, bf16[256,128,32]{1,0,2:T(8,128)(2,1)S(1)} %copy-done.13), kind=kOutput, calls=%fused_computation.49 | convolution fusion | flops 273973248 | bytes 27262976 | tf_op jit(solution)/shard_map/gb,kbw->kgw/dot_general | solution.py:48
  211.5 11.0 %add_subtract_fusion.5 = f32[256,32,128]{2,0,1:T(8,128)} fusion(f32[256,32,128]{2,0,1:T(8,128)} %fusion.158, f32[256,32,128]{2,0,1:T(8,128)} %fusion.156, f32[256,32,128]{2,0,1:T(8,128)} %fusion.261, f32[256,32,128]{2,0,1:T(8,128)} %fusion.206, f32[256,32,128]{2,0,1:T(8,128)} %fusion.204, bf16[256,128,32]{1,0,2:T(8,128)(2,1)S(1)} %copy-done.12), kind=kOutput, calls=%fused_computation.62 | convolution fusion | flops 273973248 | bytes 27262976 | tf_op jit(solution)/shard_map/gb,kbw->kgw/dot_general | solution.py:48
  223.7 3.8 add_add_fusion.5
  227.5 22.2 %multiply_add_fusion.1 = (f32[256,32,128]{2,0,1:T(8,128)}, f32[256,32,128]{2,0,1:T(8,128)}, f32[256,32,128]{2,0,1:T(8,128)}, f32[256,32,128]{2,0,1:T(8,128)}, f3...) fusion(f32[256,32,128]{2,0,1:T(8,128)} %add_subtract_fusion.2, f32[256,32,128]{2,0,1:T(8,128)} %add_add_fusion.4, ...), kind=kOutput, calls=%fused_computation.41 | convolution fusion | flops 292847616 | bytes 69206016 | tf_op jit(solution)/shard_map/gb,kbw->kgw/dot_general | solution.py:48
  249.7 5.2 %fusion.126 = f32[256,32,128]{2,0,1:T(8,128)} fusion(f32[256,32,128]{2,0,1:T(8,128)} %get-tuple-element.35), kind=kOutput, calls=%fused_computation.211 | convolution fusion | flops 268681216 | bytes 8388608 | tf_op jit(solution)/shard_map/gb,kbw->kgw/dot_general | solution.py:46
  334.9 3.4 fusion.170
  341.2 10.6 %add_subtract_fusion = f32[256,32,128]{2,0,1:T(8,128)} fusion(f32[256,32,128]{2,0,1:T(8,128)} %fusion.126, f32[256,32,128]{2,0,1:T(8,128)} %fusion.124, f32[256,32,128]{2,0,1:T(8,128)} %fusion.245, f32[256,32,128]{2,0,1:T(8,128)} %fusion.174, f32[256,32,128]{2,0,1:T(8,128)} %fusion.172, f32[256,32,128]{2,0,1:T(8,128)S(1)} %copy-done.3), kind=kOutput, calls=%fused_computation.39 | convolution fusion | flops 273973248 | bytes 29360128 | tf_op jit(solution)/shard_map/gb,kbw->kgw/dot_general | solution.py:48
  351.8 10.6 %add_subtract_fusion.1 = f32[256,32,128]{2,0,1:T(8,128)} fusion(f32[256,32,128]{2,0,1:T(8,128)} %fusion.134, f32[256,32,128]{2,0,1:T(8,128)} %fusion.132, f32[256,32,128]{2,0,1:T(8,128)} %fusion.249, f32[256,32,128]{2,0,1:T(8,128)} %fusion.182, f32[256,32,128]{2,0,1:T(8,128)} %fusion.180, f32[256,32,128]{2,0,1:T(8,128)S(1)} %copy-done.2), kind=kOutput, calls=%fused_computation.45 | convolution fusion | flops 273973248 | bytes 29360128 | tf_op jit(solution)/shard_map/gb,kbw->kgw/dot_general | solution.py:48
  362.4 10.8 %add_add_fusion.1 = f32[256,32,128]{2,0,1:T(8,128)} fusion(f32[256,32,128]{2,0,1:T(8,128)} %fusion.130, f32[256,32,128]{2,0,1:T(8,128)} %fusion.128, f32[256,32,128]{2,0,1:T(8,128)} %fusion.247, f32[256,32,128]{2,0,1:T(8,128)} %fusion.178, f32[256,32,128]{2,0,1:T(8,128)} %fusion.176, f32[256,32,128]{2,0,1:T(8,128)S(1)} %copy-done.1), kind=kOutput, calls=%fused_computation.44 | convolution fusion | flops 273973248 | bytes 29360128 | tf_op jit(solution)/shard_map/gb,kbw->kgw/dot_general | solution.py:48
  373.2 9.7 %add_subtract_fusion.3 = f32[256,32,128]{2,0,1:T(8,128)} fusion(f32[256,32,128]{2,0,1:T(8,128)S(1)} %copy-done.30, f32[256,32,128]{2,0,1:T(8,128)} %fusion.148, f32[256,32,128]{2,0,1:T(8,128)} %fusion.257, f32[256,32,128]{2,0,1:T(8,128)} %fusion.198, f32[256,32,128]{2,0,1:T(8,128)} %fusion.196, f32[256,32,128]{2,0,1:T(8,128)S(1)} %copy-done), kind=kOutput, calls=%fused_computation.58 | convolution fusion | flops 273973248 | bytes 29360128 | tf_op jit(solution)/shard_map/gb,kbw->kgw/dot_general | solution.py:48
  383.0 8.8 %add_add_fusion.3 = f32[256,32,128]{2,0,1:T(8,128)} fusion(f32[256,32,128]{2,0,1:T(8,128)S(1)} %copy-done.28, f32[256,32,128]{2,0,1:T(8,128)S(1)} %copy-done.29, f32[256,32,128]{2,0,1:T(8,128)} %fusion.255, f32[256,32,128]{2,0,1:T(8,128)} %fusion.194, f32[256,32,128]{2,0,1:T(8,128)} %fusion.192, f32[256,32,128]{2,0,1:T(8,128)S(1)} %get-tuple-element.55), kind=kOutput, calls=%fused_computation.57 | convolution fusion | flops 273973248 | bytes 29360128 | tf_op jit(solution)/shard_map/gb,kbw->kgw/dot_general | solution.py:48
  391.7 21.4 %bitcast_convert_fusion.1 = (bf16[256,128,32]{1,0,2:T(8,128)(2,1)}, bf16[256,128,32]{1,0,2:T(8,128)(2,1)S(1)}, bf16[256,128,32]{1,0,2:T(8,128)(2,1)}, bf16[256,1...) fusion(f32[256,128]{1,0:T(8,128)S(1)} %copy-done.38, ...), kind=kOutput, calls=%fused_computation.4 | convolution fusion | flops 299139072 | bytes 63176704 | tf_op jit(solution)/shard_map/gb,kbw->kgw/dot_general | solution.py:48
  439.3 4.7 all-to-all-start.1
  444.0 8.8 %multiply_convert_fusion = bf16[128,128,32]{1,0,2:T(8,128)(2,1)S(1)} fusion(f32[128,128,32]{1,0,2:T(8,128)} %fusion.685, f32[128,128,32]{1,0,2:T(8,128)} %fusion.87, f32[128,128,32]{1,0,2:T(8,128)} %fusion.684, f32[128,128,32]{1,0,2:T(8,128)} %fusion.108, f32[128,128,32]{1,0,2:T(8,128)} %fusion.21, bf16[256,128,32]{1,0,2:T(8,128)(2,1)} %get-tuple-element.58, ...), kind=kOutput, calls=%fused_computation.99 | convolution fusion | flops 278396928 | bytes 22347776 | tf_op jit(solution)/shard_map/ak,kbw->abw/dot_general | solution.py:47
  463.3 7.6 %all-to-all-start.3 = ((bf16[128,128,32]{1,2,0:T(8,128)(2,1)}), bf16[128,128,32]{1,2,0:T(8,128)(2,1)}, u32[]{:S(2)}, u32[]{:S(2)}) async-start(bf16[128,128,32]{1,2,0:T(8,128)(2,1)} %copy.27), calls=%async_computation.3 | async-start | bytes 2097152 | tf_op jit(solution)/shard_map/all_to_all | solution.py:120
  470.9 8.0 %subtract_multiply_fusion = f32[128,128,32]{1,0,2:T(8,128)S(1)} fusion(f32[128,128,32]{1,0,2:T(8,128)} %fusion.687, f32[128,128,32]{1,0,2:T(8,128)} %fusion.84, f32[128,128,32]{1,0,2:T(8,128)} %fusion.686, f32[128,128,32]{1,0,2:T(8,128)} %fusion.105, f32[128,128,32]{1,0,2:T(8,128)} %fusion.25, bf16[256,128,32]{1,0,2:T(8,128)(2,1)S(1)} %get-tuple-element.41, ...), kind=kOutput, calls=%fused_computation.98 | convolution fusion | flops 277872640 | bytes 23396352 | tf_op jit(solution)/shard_map/ak,kbw->abw/dot_general | solution.py:47
  485.0 4.9 all-to-all-done.3
  (226 shorter events, 259.2 us)
Async XLA Ops:
  4.3 17.2 %copy-start.43 = (bf16[128,4096]{0,1:T(8,128)(2,1)}, bf16[128,4096]{0,1:T(8,128)(2,1)S(1)}, u32[]{:S(2)}) copy-start(bf16[128,4096]{0,1:T(8,128)(2,1)S(1)} %copy.21) | copy-start | bytes 3145732
  5.6 30.8 %all-to-all-start = ((bf16[128,128,32]{0,2,1:T(8,128)(2,1)}), bf16[128,128,32]{0,2,1:T(8,128)(2,1)S(1)}, u32[]{:S(2)}, u32[]{:S(2)}) async-start(bf16[128,128,32]{0,2,1:T(8,128)(2,1)} %bitcast.9), calls=%async_computation | async-start | bytes 2097152 | tf_op jit(solution)/shard_map/all_to_all | solution.py:105
  19.6 58.8 %copy-start.37 = (f32[256,128]{1,0:T(8,128)}, f32[256,128]{1,0:T(8,128)S(1)}, u32[]{:S(2)}) copy-start(f32[256,128]{1,0:T(8,128)S(1)} %get-tuple-element.71) | copy-start | bytes 393220
  32.7 18.5 %copy-start.45 = (bf16[128,4096]{0,1:T(8,128)(2,1)}, bf16[128,4096]{0,1:T(8,128)(2,1)S(1)}, u32[]{:S(2)}) copy-start(bf16[128,4096]{0,1:T(8,128)(2,1)S(1)} %copy.20) | copy-start | bytes 3145732
  36.4 29.1 %all-to-all-start.2 = ((bf16[128,128,32]{0,2,1:T(8,128)(2,1)}), bf16[128,128,32]{0,2,1:T(8,128)(2,1)S(1)}, u32[]{:S(2)}, u32[]{:S(2)}) async-start(bf16[128,128,32]{0,2,1:T(8,128)(2,1)} %bitcast.656), calls=%async_computation.2 | async-start | bytes 2097152 | tf_op jit(solution)/shard_map/all_to_all | solution.py:106
  46.8 31.6 %copy-start.39 = (f32[256,128]{1,0:T(8,128)}, f32[256,128]{1,0:T(8,128)S(1)}, u32[]{:S(2)}) copy-start(f32[256,128]{1,0:T(8,128)S(1)} %fusion.116) | copy-start | bytes 393220
  53.9 15.1 %copy-start.56 = (bf16[256,128,1]{1,0,2:T(8,128)(2,1)S(1)}, bf16[256,128,1]{1,0,2:T(8,128)(2,1)}, u32[]{:S(2)}) copy-start(bf16[256,128,1]{1,0,2:T(8,128)(2,1)} %copy-done.55) | copy-start | bytes 196612
  191.9 10.9 %copy-start.33 = (f32[256,32,128]{2,0,1:T(8,128)S(1)}, f32[256,32,128]{2,0,1:T(8,128)}, u32[]{:S(2)}) copy-start(f32[256,32,128]{2,0,1:T(8,128)} %fusion.140) | copy-start | bytes 12582916
  211.5 11.0 %copy-start.34 = (f32[256,32,128]{2,0,1:T(8,128)S(1)}, f32[256,32,128]{2,0,1:T(8,128)}, u32[]{:S(2)}) copy-start(f32[256,32,128]{2,0,1:T(8,128)} %fusion.265) | copy-start | bytes 12582916
  211.5 11.0 %copy-start.35 = (f32[256,32,128]{2,0,1:T(8,128)S(1)}, f32[256,32,128]{2,0,1:T(8,128)}, u32[]{:S(2)}) copy-start(f32[256,32,128]{2,0,1:T(8,128)} %fusion.214) | copy-start | bytes 12582916
  211.5 12.2 %copy-start.36 = (f32[256,32,128]{2,0,1:T(8,128)S(1)}, f32[256,32,128]{2,0,1:T(8,128)}, u32[]{:S(2)}) copy-start(f32[256,32,128]{2,0,1:T(8,128)} %fusion.212) | copy-start | bytes 12582916
  362.4 10.8 %copy-start.30 = (f32[256,32,128]{2,0,1:T(8,128)S(1)}, f32[256,32,128]{2,0,1:T(8,128)}, u32[]{:S(2)}) copy-start(f32[256,32,128]{2,0,1:T(8,128)} %fusion.150) | copy-start | bytes 12582916
  373.2 9.7 %copy-start.28 = (f32[256,32,128]{2,0,1:T(8,128)S(1)}, f32[256,32,128]{2,0,1:T(8,128)}, u32[]{:S(2)}) copy-start(f32[256,32,128]{2,0,1:T(8,128)} %fusion.146) | copy-start | bytes 12582916
  373.2 9.7 %copy-start.29 = (f32[256,32,128]{2,0,1:T(8,128)S(1)}, f32[256,32,128]{2,0,1:T(8,128)}, u32[]{:S(2)}) copy-start(f32[256,32,128]{2,0,1:T(8,128)} %fusion.144) | copy-start | bytes 12582916
  382.9 8.8 %copy-start.5 = (f32[256,32,128]{2,0,1:T(8,128)S(1)}, f32[256,32,128]{2,0,1:T(8,128)}, u32[]{:S(2)}) copy-start(f32[256,32,128]{2,0,1:T(8,128)} %get-tuple-element.34) | copy-start | bytes 12582916
  382.9 8.8 %copy-start.38 = (f32[256,128]{1,0:T(8,128)S(1)}, f32[256,128]{1,0:T(8,128)}, u32[]{:S(2)}) copy-start(f32[256,128]{1,0:T(8,128)} %copy-done.37) | copy-start | bytes 393220
  391.7 21.4 %copy-start.48 = (bf16[128,256]{1,0:T(8,128)(2,1)S(1)}, bf16[128,256]{1,0:T(8,128)(2,1)}, u32[]{:S(2)}) copy-start(bf16[128,256]{1,0:T(8,128)(2,1)} %get-tuple-element.17) | copy-start | bytes 196612
  391.7 23.6 %copy-start.10 = (f32[256,32,128]{2,0,1:T(8,128)S(1)}, f32[256,32,128]{2,0,1:T(8,128)}, u32[]{:S(2)}) copy-start(f32[256,32,128]{2,0,1:T(8,128)} %add_add_fusion.3) | copy-start | bytes 12582916
  439.3 24.0 %all-to-all-start.1 = ((bf16[128,128,32]{1,2,0:T(8,128)(2,1)}), bf16[128,128,32]{1,2,0:T(8,128)(2,1)S(1)}, u32[]{:S(2)}, u32[]{:S(2)}) async-start(bf16[128,128,32]{1,2,0:T(8,128)(2,1)} %copy.24), calls=%async_computation.1 | async-start | bytes 2097152 | tf_op jit(solution)/shard_map/all_to_all | solution.py:119
  444.0 8.8 %copy-start.17 = (bf16[256,128,32]{1,0,2:T(8,128)(2,1)S(1)}, bf16[256,128,32]{1,0,2:T(8,128)(2,1)}, u32[]{:S(2)}) copy-start(bf16[256,128,32]{1,0,2:T(8,128)(2,1)} %get-tuple-element.40) | copy-start | bytes 6291460
  444.0 8.8 %copy-start.51 = (bf16[128,256,1]{1,0,2:T(8,128)(2,1)S(1)}, bf16[128,256,1]{1,0,2:T(8,128)(2,1)}, u32[]{:S(2)}) copy-start(bf16[128,256,1]{1,0,2:T(8,128)(2,1)} %get-tuple-element.16) | copy-start | bytes 196612
  463.3 26.6 %all-to-all-start.3 = ((bf16[128,128,32]{1,2,0:T(8,128)(2,1)}), bf16[128,128,32]{1,2,0:T(8,128)(2,1)}, u32[]{:S(2)}, u32[]{:S(2)}) async-start(bf16[128,128,32]{1,2,0:T(8,128)(2,1)} %copy.27), calls=%async_computation.3 | async-start | bytes 2097152 | tf_op jit(solution)/shard_map/all_to_all | solution.py:120
  478.9 11.0 %copy-start.42 = (bf16[128,4096]{0,1:T(8,128)(2,1)S(1)}, bf16[128,4096]{0,1:T(8,128)(2,1)}, u32[]{:S(2)}) copy-start(bf16[128,4096]{0,1:T(8,128)(2,1)} %copy-done.41) | copy-start | bytes 3145732
  479.0 11.0 %copy-start.44 = (bf16[128,4096]{0,1:T(8,128)(2,1)S(1)}, bf16[128,4096]{0,1:T(8,128)(2,1)}, u32[]{:S(2)}) copy-start(bf16[128,4096]{0,1:T(8,128)(2,1)} %copy-done.43) | copy-start | bytes 3145732
  (37 other events, 126.2 us)
where the time goes:
time: 504 us; the launch traced here: 496 us
  matrix products  402 us (80%)
  starting transfers between devices  33.6 us (7%)
  local copies, waits for them, and re-layouts  26.2 us (5%)
  waiting for transfers between devices  19.7 us (4%)
  other arithmetic  13.9 us (3%)
    dot_general x32, matrix products, mixed(): jnp.einsum(form, lower, data_upper, preferred_element_type=jnp.float32)  190 us
    dot_general x32, matrix products, mixed(): jnp.einsum(form, upper, data_lower, preferred_element_type=jnp.float32)  97.3 us
    dot_general x32, matrix products, mixed(): jnp.einsum(form, upper, data_upper, preferred_element_type=jnp.float32)  80.7 us
    dot_general x4, matrix products, mixed(): jnp.einsum(form, lower, data, preferred_element_type=jnp.float32)  24.4 us
    unnamed x123, local copies, waits for them, and re-layouts  22.9 us
    all_to_all x1, waiting for transfers between devices, local(): lax.all_to_all(gated_grad, ('dp', 'ctx'), split_axis=1, concat_axis=0, ti...  11.6 us
    all_to_all x1, starting transfers between devices, local(): lax.all_to_all(gated, ('dp', 'ctx'), split_axis=1, concat_axis=0, tiled=T...  11.5 us
  transfers between devices with their start and end apart: 4, of which 4 were waited for; matrix products, arithmetic and copies ran while one was open for 11% of the time, Pallas kernels for 0%

commit v1 on v0

v1 whole, which is shorter than its diff:
```python
import functools
import math

import jax
import jax.numpy as jnp
import numpy as np
from jax import lax
from jax.experimental import pallas as pl
from jax.experimental.pallas import tpu as pltpu
from jax.sharding import PartitionSpec as P

MESH = pl.DeviceIdType.MESH
F32 = jnp.float32
BF16 = jnp.bfloat16
N = 128
W = 32
C = N * W
GROUP = 4


def make_tables():
    a = np.arange(128, dtype=np.float64)
    k = np.arange(128, dtype=np.float64)
    outer = 2.0 * np.pi * np.outer(k + 0.5, a) / 256.0
    first = np.concatenate([np.cos(outer), -np.sin(outer)], axis=0)
    last = first.T * (2.0 / 32768.0 / 128.0)
    inner = 2.0 * np.pi * (np.outer(a, a) % 128) / 128.0
    c, s = np.cos(inner), np.sin(inner)
    second = np.block([[c, -s], [s, c]])
    twist = 2.0 * np.pi * np.outer(k + 0.5, a) / 32768.0
    index = np.arange(256)
    swap = np.zeros((256, 256))
    swap[index, (index % 16) * 16 + index // 16] = 1.0
    wide = np.concatenate([second, second.T, np.eye(256), swap, last], axis=0)
    return (
        jnp.asarray(wide.astype(np.float32), BF16),
        jnp.asarray(first.astype(np.float32), BF16),
        jnp.asarray(np.concatenate([np.cos(twist), np.sin(twist)], axis=0), F32),
    )


def dot(x, y):
    return lax.dot_general(x, y, (((1,), (0,)), ((), ())), preferred_element_type=F32)


def dot_nt(x, y):
    return lax.dot_general(x, y, (((1,), (1,)), ((), ())), preferred_element_type=F32)


def kernel(
    q_hbm, k_hbm, v_hbm, g_hbm, taps_hbm, wide_hbm, first_hbm, twist_hbm,
    qg_ref, kg_ref, vg_ref, fg_ref,
    q, k, v, g, taps, wide, first, twist,
    send, recv, xt, spec_h, spec_g, spec_q,
    load_sem, send_sem, recv_sem, own_sem,
):
    dp, ctx = lax.axis_index("dp"), lax.axis_index("ctx")
    me = dp * 16 + ctx
    cx, cy, cz, cc = (dp % 2) * 2 + (ctx // 2) % 2, ctx // 4, dp // 2, ctx % 2

    loads = [
        pltpu.make_async_copy(src, dst, load_sem.at[i])
        for i, (src, dst) in enumerate(
            [(wide_hbm, wide), (k_hbm, k), (v_hbm, v), (q_hbm, q), (g_hbm, g),
             (first_hbm, first), (twist_hbm, twist), (taps_hbm, taps)]
        )
    ]
    for load in loads:
        load.start()

    def partner(i):
        x = (cx + i) % 4
        y = (cy + i // 4 + i) % 4
        z = (cz + i // 16 + i // 4 + i) % 4
        c = (cc + i // 64 + i) % 2
        return z * 2 + x // 2, y * 4 + (x % 2) * 2 + c

    barrier = pltpu.get_barrier_semaphore()

    @pl.loop(1, N)
    def _(i):
        pl.semaphore_signal(barrier, inc=1, device_id=partner(i), device_id_type=MESH)

    ident = wide.at[512:768]
    swap = wide.at[768:1024]

    def gate_in(left, right, slot):
        @pl.loop(0, C // 256)
        def _(i):
            cols = pl.ds(pl.multiple_of(i * 256, 256), 256)
            gated = (left[:, cols].astype(F32) * right[:, cols].astype(F32)).astype(BF16)
            turned = dot_nt(ident[...], gated).astype(BF16)
            send[slot, pl.ds(pl.multiple_of(i * 8, 8), 8)] = turned.reshape(8, W, 128)

    for load in loads[:3]:
        load.wait()
    gate_in(k, v, 0)
    for load in loads[3:5]:
        load.wait()
    gate_in(g, q, 1)
    pl.semaphore_wait(barrier, N - 1)

    def start_sends(slot):
        @pl.loop(1, N)
        def _(i):
            d, e = partner(i)
            pltpu.make_async_remote_copy(
                src_ref=send.at[slot, d * 16 + e],
                dst_ref=recv.at[slot, me],
                send_sem=send_sem.at[slot],
                recv_sem=recv_sem.at[slot],
                device_id=(d, e),
                device_id_type=MESH,
            ).start()

        pltpu.make_async_copy(send.at[slot, me], recv.at[slot, me], own_sem.at[slot]).start()

    def wait_recv(slot):
        others = recv.at[slot, pl.ds(0, N - 1)]
        pltpu.make_async_copy(others, others, recv_sem.at[slot]).wait()
        pltpu.make_async_copy(send.at[slot, me], recv.at[slot, me], own_sem.at[slot]).wait()

    def wait_send(slot):
        others = send.at[slot, pl.ds(0, N - 1)]
        pltpu.make_async_copy(others, others, send_sem.at[slot]).wait()

    start_sends(0)
    start_sends(1)
    for load in loads[5:]:
        load.wait()

    cos, sin = twist.at[0:128], twist.at[128:256]

    def swap_blocks(load_block, store_block):
        @pl.loop(0, 8)
        def _(i):
            for j in range(2):
                store_block(i, j, dot(swap[...], load_block(i, j)))

    def recv_block(slot):
        def load(i, j):
            rows = recv[slot, pl.ds(pl.multiple_of(i * 16, 16), 16), pl.ds(j * 16, 16), :]
            return rows.reshape(256, 128)

        return load

    def taps_block(i, j):
        parts = []
        for s in range(16):
            lanes = pl.ds(pl.multiple_of((i * 16 + s) * 128, 128), 128)
            parts.append(taps[pl.ds(j * 16, 16), lanes])
        return jnp.concatenate(parts, axis=0).astype(BF16)

    def xt_store(i, j, block):
        rows = pl.ds(pl.multiple_of(i * 16, 16), 16)
        xt[pl.ds(j * 16, 16), rows, :] = block.astype(BF16).reshape(16, 16, 128)

    def xt_block(i, j):
        rows = pl.ds(pl.multiple_of(i * 16, 16), 16)
        return xt[pl.ds(j * 16, 16), rows, :].reshape(256, 128)

    def send_store(slot):
        def store(i, j, block):
            rows = pl.ds(pl.multiple_of(i * 16, 16), 16)
            send[slot, rows, pl.ds(j * 16, 16), :] = block.astype(BF16).reshape(16, 16, 128)

        return store

    def fg_store(i, j, block):
        for s in range(16):
            lanes = pl.ds(pl.multiple_of((i * 16 + s) * 128, 128), 128)
            fg_ref[pl.ds(j * 16, 16), lanes] = block[s * 16 : (s + 1) * 16]

    def forward(ws):
        outer = [dot(first[...], xt[w]) for w in ws]
        twisted = []
        for x in outer:
            re, im = x[:128], x[128:]
            c, s = cos[...], sin[...]
            twisted.append(
                jnp.concatenate([re * c + im * s, im * c - re * s], axis=1).astype(BF16)
            )
        return [dot(x, wide[0:256]) for x in twisted]

    def backward(ws, products):
        inner = [dot(x, wide[256:512]) for x in products]
        twisted = []
        for x in inner:
            re, im = x[:, :128], x[:, 128:]
            c, s = cos[...], sin[...]
            twisted.append(
                jnp.concatenate([re * c - im * s, re * s + im * c], axis=0).astype(BF16)
            )
        for w, x in zip(ws, twisted):
            xt[w] = dot(wide[1024:1152], x).astype(BF16)

    def product(x, y):
        xr, xi, yr, yi = x[:, :128], x[:, 128:], y[:, :128], y[:, 128:]
        return jnp.concatenate([xr * yr - xi * yi, xr * yi + xi * yr], axis=1).astype(BF16)

    def conj_product(x, y):
        xr, xi, yr, yi = x[:, :128], x[:, 128:], y[:, :128], y[:, 128:]
        return jnp.concatenate([xr * yr + xi * yi, xr * yi - xi * yr], axis=1).astype(BF16)

    def groups(body):
        @pl.loop(0, W // GROUP)
        def _(i):
            body([i * GROUP + j for j in range(GROUP)])

    swap_blocks(taps_block, xt_store)

    def taps_step(ws):
        for w, x in zip(ws, forward(ws)):
            spec_h[w] = x.astype(BF16)

    groups(taps_step)

    wait_recv(0)
    swap_blocks(recv_block(0), xt_store)

    def gated_step(ws):
        found = forward(ws)
        for w, x in zip(ws, found):
            spec_g[w] = x.astype(BF16)
        backward(ws, [product(x, spec_h[w].astype(F32)) for w, x in zip(ws, found)])

    groups(gated_step)
    swap_blocks(xt_block, send_store(2))
    start_sends(2)

    wait_recv(1)
    swap_blocks(recv_block(1), xt_store)

    def grad_step(ws):
        found = forward(ws)
        for w, x in zip(ws, found):
            spec_q[w] = x.astype(BF16)
        backward(ws, [conj_product(spec_h[w].astype(F32), x) for w, x in zip(ws, found)])

    groups(grad_step)
    swap_blocks(xt_block, send_store(3))
    start_sends(3)

    def filter_step(ws):
        backward(ws, [conj_product(spec_g[w].astype(F32), spec_q[w].astype(F32)) for w in ws])

    groups(filter_step)
    swap_blocks(xt_block, fg_store)

    def turned(slot, i):
        rows = recv[slot, pl.ds(pl.multiple_of(i * 8, 8), 8)].reshape(256, 128)
        return dot_nt(wide[512:640, 0:128], rows)

    wait_recv(2)

    @pl.loop(0, C // 256)
    def _(i):
        cols = pl.ds(pl.multiple_of(i * 256, 256), 256)
        qg_ref[:, cols] = (g[:, cols].astype(F32) * turned(2, i)).astype(BF16)

    wait_recv(3)

    @pl.loop(0, C // 256)
    def _(i):
        cols = pl.ds(pl.multiple_of(i * 256, 256), 256)
        back = turned(3, i)
        kg_ref[:, cols] = (v[:, cols].astype(F32) * back).astype(BF16)
        vg_ref[:, cols] = (k[:, cols].astype(F32) * back).astype(BF16)

    for slot in range(4):
        wait_send(slot)


def local(queries, keys, values, grad_out, filter_param):
    wide, first, twist = make_tables()
    hbm = pl.BlockSpec(memory_space=pltpu.HBM)
    vmem = pl.BlockSpec(memory_space=pltpu.VMEM)
    rows = (N, C)
    out = pl.pallas_call(
        kernel,
        out_shape=[jax.ShapeDtypeStruct(rows, BF16)] * 3
        + [jax.ShapeDtypeStruct((W, N * N), F32)],
        in_specs=[hbm] * 8,
        out_specs=[vmem] * 4,
        scratch_shapes=[
            pltpu.VMEM(rows, BF16),
            pltpu.VMEM(rows, BF16),
            pltpu.VMEM(rows, BF16),
            pltpu.VMEM(rows, BF16),
            pltpu.VMEM((W, N * N), F32),
            pltpu.VMEM(wide.shape, BF16),
            pltpu.VMEM(first.shape, BF16),
            pltpu.VMEM(twist.shape, F32),
            pltpu.VMEM((4, N, W, 128), BF16),
            pltpu.VMEM((4, N, W, 128), BF16),
            pltpu.VMEM((W, 128, 128), BF16),
            pltpu.VMEM((W, 128, 256), BF16),
            pltpu.VMEM((W, 128, 256), BF16),
            pltpu.VMEM((W, 128, 256), BF16),
            pltpu.SemaphoreType.DMA((8,)),
            pltpu.SemaphoreType.DMA((4,)),
            pltpu.SemaphoreType.DMA((4,)),
            pltpu.SemaphoreType.DMA((4,)),
        ],
        compiler_params=pltpu.CompilerParams(
            collective_id=0, has_side_effects=True, vmem_limit_bytes=48 << 20
        ),
        cost_estimate=pl.CostEstimate(flops=5 << 30, bytes_accessed=11 << 20, transcendentals=0),
    )(queries, keys, values, grad_out, filter_param.T, wide, first, twist)
    query_grad, key_grad, value_grad, filter_grad = out
    return query_grad, key_grad, value_grad, filter_grad.T


def solution(mesh):
    split = P(("dp", "ctx"), None)
    channels = P(None, ("dp", "ctx"))
    return jax.shard_map(
        local,
        mesh=mesh,
        in_specs=(split, split, split, split, channels),
        out_specs=(split, split, split, channels),
        check_vma=False,
    )
```

time: 504 us -> 86.9 us (0.17); the launches traced: 496 us -> 85.8 us
  matrix products: 402 us -> 0 us
  Pallas kernels: 0 us -> 75.6 us
  starting transfers between devices: 33.6 us -> 0 us
  waiting for transfers between devices: 19.7 us -> 0 us
  local copies, waits for them, and re-layouts: 26.2 us -> 9.55 us
  other arithmetic: 13.9 us -> 0 us
    dot_general x104 -> x0, matrix products: 402 us -> none  [the longest x32 190 us: mixed(): jnp.einsum(form, lower, data_upper, preferred_element_type=jnp.float32)]
    pallas_call x0 -> x1, Pallas kernels: none -> 75.6 us  [local(): pl.pallas_call(kernel, out_shape=[jax.ShapeDtypeStruct(rows, BF16)] * 3 +...]
    all_to_all x4 -> x0, starting transfers between devices: 33.6 us -> none  [the longest x1 11.5 us: local(): lax.all_to_all(gated, ('dp', 'ctx'), split_axis=1, concat_axis=0, tiled=T...]
    all_to_all x4 -> x0, waiting for transfers between devices: 19.7 us -> none  [the longest x1 11.6 us: local(): lax.all_to_all(gated_grad, ('dp', 'ctx'), split_axis=1, concat_axis=0, ti...]
    unnamed x123 -> x16, local copies, waits for them, and re-layouts: 22.9 us -> 9.55 us
    convert_element_type x9 -> x0, other arithmetic: 9.63 us -> none  [the longest x5 3.17 us: split_parts(): lower = (array - upper.astype(jnp.float32)).astype(jnp.bfloat16)]
  transfers between devices with their start and end apart: 4 -> 0, of which waited for: 4 -> 0; matrix products, arithmetic and copies ran while one was open for 11% -> 0% of each run, Pallas kernels for 0% -> 0%
where the time goes in v1:
time: 86.9 us; the launch traced here: 85.8 us
  Pallas kernels  75.6 us (87%)
  local copies, waits for them, and re-layouts  9.55 us (11%)
    pallas_call x1, Pallas kernels, local(): pl.pallas_call(kernel, out_shape=[jax.ShapeDtypeStruct(rows, BF16)] * 3 +...  75.6 us
    unnamed x16, local copies, waits for them, and re-layouts  9.55 us

profile of v1, /device:TPU:1, one launch (start us, length us, event | category | flops | bytes accessed | tf_op | source)
XLA Modules:
  0.0 85.8 jit_solution(1552774012618170358)
XLA Ops:
  0.6 0.0 copy-start
  0.6 1.2 %copy-done = bf16[128,4096]{1,0:T(8,128)(2,1)S(1)} copy-done((bf16[128,4096]{1,0:T(8,128)(2,1)S(1)}, bf16[128,4096]{1,0:T(8,128)(2,1)}, u32[]{:S(2)}) %copy-start) | copy-done | bytes 1048600
  1.9 0.0 copy-start.1
  1.9 1.2 %copy-done.1 = bf16[128,4096]{1,0:T(8,128)(2,1)S(1)} copy-done((bf16[128,4096]{1,0:T(8,128)(2,1)S(1)}, bf16[128,4096]{1,0:T(8,128)(2,1)}, u32[]{:S(2)}) %copy-start.1) | copy-done | bytes 1048600
  3.1 0.0 copy-start.2
  3.1 1.1 %copy-done.2 = bf16[1152,256]{1,0:T(8,128)(2,1)S(1)} copy-done((bf16[1152,256]{1,0:T(8,128)(2,1)S(1)}, bf16[1152,256]{1,0:T(8,128)(2,1)}, u32[]{:S(2)}) %copy-start.2) | copy-done | bytes 589848
  4.1 0.0 copy-start.3
  4.2 0.9 %copy-done.3 = f32[256,128]{1,0:T(8,128)S(1)} copy-done((f32[256,128]{1,0:T(8,128)S(1)}, f32[256,128]{1,0:T(8,128)}, u32[]{:S(2)}) %copy-start.3) | copy-done | bytes 131096
  5.1 0.0 copy-start.4
  5.1 0.8 copy-done.4
  5.9 75.6 %shard_map.111 = (bf16[128,4096]{1,0:T(8,128)(2,1)S(1)}, bf16[128,4096]{1,0:T(8,128)(2,1)S(1)}, bf16[128,4096]{1,0:T(8,128)(2,1)S(1)}, f32[32,16384]{1,0:T(8,128)}) custom-call(bf16[128,4096]{1,0:T(8,128)(2,1)S(1)} %copy-done, bf16[128,4096]{1,0:T(8,128)(2,1)S(1)} %copy-done.1, bf16[128,4096]{1,0:T(8,128)(2,1)} %v_hbm.1, bf16[128,4096]{1,0:T(8,128)(2,1)} %g_hbm.1, ...), custom_call_target="tpu_custom_call" | custom-call | flops 5368709120 | bytes 11534336 | tf_op jit(solution)/shard_map/pallas_call | solution.py:279
  81.5 1.0 %copy.16 = bf16[128,4096]{1,0:T(8,128)(2,1)} copy(bf16[128,4096]{1,0:T(8,128)(2,1)S(1)} %get-tuple-element.16) | data formatting | bytes 2097152
  82.5 0.0 copy-start.5
  82.5 1.0 %copy.17 = bf16[128,4096]{1,0:T(8,128)(2,1)} copy(bf16[128,4096]{1,0:T(8,128)(2,1)S(1)} %get-tuple-element.17) | data formatting | bytes 2097152
  83.5 1.0 %copy.18 = bf16[128,4096]{1,0:T(8,128)(2,1)} copy(bf16[128,4096]{1,0:T(8,128)(2,1)S(1)} %get-tuple-element.18) | data formatting | bytes 2097152
  84.4 0.1 copy-done.5
  84.5 1.3 %copy.19 = f32[16384,32]{0,1:T(8,128)} copy(f32[16384,32]{0,1:T(8,128)S(1)} %bitcast.2) | data formatting | bytes 4194304
Async XLA Ops:
  0.6 1.2 %copy-start = (bf16[128,4096]{1,0:T(8,128)(2,1)S(1)}, bf16[128,4096]{1,0:T(8,128)(2,1)}, u32[]{:S(2)}) copy-start(bf16[128,4096]{1,0:T(8,128)(2,1)} %q_hbm.1) | copy-start | bytes 3145732
  1.9 1.2 %copy-start.1 = (bf16[128,4096]{1,0:T(8,128)(2,1)S(1)}, bf16[128,4096]{1,0:T(8,128)(2,1)}, u32[]{:S(2)}) copy-start(bf16[128,4096]{1,0:T(8,128)(2,1)} %k_hbm.1) | copy-start | bytes 3145732
  3.1 1.1 %copy-start.2 = (bf16[1152,256]{1,0:T(8,128)(2,1)S(1)}, bf16[1152,256]{1,0:T(8,128)(2,1)}, u32[]{:S(2)}) copy-start(bf16[1152,256]{1,0:T(8,128)(2,1)} %constant.6.clone.wide_hbm) | copy-start | bytes 1769476
  4.1 0.9 %copy-start.3 = (f32[256,128]{1,0:T(8,128)S(1)}, f32[256,128]{1,0:T(8,128)}, u32[]{:S(2)}) copy-start(f32[256,128]{1,0:T(8,128)} %constant.8.clone.twist_hbm) | copy-start | bytes 393220
  5.1 0.8 copy-start.4
  82.5 2.0 %copy-start.5 = (f32[32,16384]{1,0:T(8,128)S(1)}, f32[32,16384]{1,0:T(8,128)}, u32[]{:S(2)}) copy-start(f32[32,16384]{1,0:T(8,128)} %get-tuple-element.11) | copy-start | bytes 6291460

commit v2 on v1

--- a/solution.py
+++ b/solution.py
@@ -16,6 +16,8 @@
 W = 32
 C = N * W
 GROUP = 4
+UNROLL = 4
+SWAP_UNROLL = 2
 
 
 def make_tables():
@@ -85,19 +87,19 @@
     swap = wide.at[768:1024]
 
     def gate_in(left, right, slot):
-        @pl.loop(0, C // 256)
-        def _(i):
-            cols = pl.ds(pl.multiple_of(i * 256, 256), 256)
-            gated = (left[:, cols].astype(F32) * right[:, cols].astype(F32)).astype(BF16)
-            turned = dot_nt(ident[...], gated).astype(BF16)
-            send[slot, pl.ds(pl.multiple_of(i * 8, 8), 8)] = turned.reshape(8, W, 128)
+        @pl.loop(0, C // 256 // UNROLL)
+        def _(i):
+            turned = []
+            for u in range(UNROLL):
+                cols = pl.ds(pl.multiple_of(i * (256 * UNROLL) + u * 256, 256), 256)
+                gated = (left[:, cols].astype(F32) * right[:, cols].astype(F32)).astype(BF16)
+                turned.append(dot_nt(ident[...], gated).astype(BF16))
+            for u in range(UNROLL):
+                send[slot, pl.ds(pl.multiple_of(i * (8 * UNROLL) + u * 8, 8), 8)] = turned[u].reshape(8, W, 128)
 
     for load in loads[:3]:
         load.wait()
     gate_in(k, v, 0)
-    for load in loads[3:5]:
-        load.wait()
-    gate_in(g, q, 1)
     pl.semaphore_wait(barrier, N - 1)
 
     def start_sends(slot):
@@ -125,6 +127,9 @@
         pltpu.make_async_copy(others, others, send_sem.at[slot]).wait()
 
     start_sends(0)
+    for load in loads[3:5]:
+        load.wait()
+    gate_in(g, q, 1)
     start_sends(1)
     for load in loads[5:]:
         load.wait()
@@ -132,10 +137,12 @@
     cos, sin = twist.at[0:128], twist.at[128:256]
 
     def swap_blocks(load_block, store_block):
-        @pl.loop(0, 8)
-        def _(i):
-            for j in range(2):
-                store_block(i, j, dot(swap[...], load_block(i, j)))
+        @pl.loop(0, 8 // SWAP_UNROLL)
+        def _(i):
+            blocks = [(i * SWAP_UNROLL + u, j) for u in range(SWAP_UNROLL) for j in range(2)]
+            found = [dot(swap[...], load_block(*block)) for block in blocks]
+            for block, x in zip(blocks, found):
+                store_block(*block, x)
 
     def recv_block(slot):
         def load(i, j):
@@ -251,21 +258,19 @@
         rows = recv[slot, pl.ds(pl.multiple_of(i * 8, 8), 8)].reshape(256, 128)
         return dot_nt(wide[512:640, 0:128], rows)
 
+    def gate_out(slot, pairs):
+        @pl.loop(0, C // 256 // UNROLL)
+        def _(i):
+            found = [turned(slot, i * UNROLL + u) for u in range(UNROLL)]
+            for u in range(UNROLL):
+                cols = pl.ds(pl.multiple_of(i * (256 * UNROLL) + u * 256, 256), 256)
+                for out_ref, gate in pairs:
+                    out_ref[:, cols] = (gate[:, cols].astype(F32) * found[u]).astype(BF16)
+
     wait_recv(2)
-
-    @pl.loop(0, C // 256)
-    def _(i):
-        cols = pl.ds(pl.multiple_of(i * 256, 256), 256)
-        qg_ref[:, cols] = (g[:, cols].astype(F32) * turned(2, i)).astype(BF16)
-
+    gate_out(2, [(qg_ref, g)])
     wait_recv(3)
-
-    @pl.loop(0, C // 256)
-    def _(i):
-        cols = pl.ds(pl.multiple_of(i * 256, 256), 256)
-        back = turned(3, i)
-        kg_ref[:, cols] = (v[:, cols].astype(F32) * back).astype(BF16)
-        vg_ref[:, cols] = (k[:, cols].astype(F32) * back).astype(BF16)
+    gate_out(3, [(kg_ref, v), (vg_ref, k)])
 
     for slot in range(4):
         wait_send(slot)
@@ -303,7 +308,7 @@
             pltpu.SemaphoreType.DMA((4,)),
         ],
         compiler_params=pltpu.CompilerParams(
-            collective_id=0, has_side_effects=True, vmem_limit_bytes=48 << 20
+            collective_id=0, has_side_effects=True, vmem_limit_bytes=62 << 20
         ),
         cost_estimate=pl.CostEstimate(flops=5 << 30, bytes_accessed=11 << 20, transcendentals=0),
     )(queries, keys, values, grad_out, filter_param.T, wide, first, twist)

time: 86.9 us -> 76.1 us (0.88); the launches traced: 85.8 us -> 75.9 us
  Pallas kernels: 75.6 us -> 69.5 us
  local copies, waits for them, and re-layouts: 9.55 us -> 5.77 us
    pallas_call x1, Pallas kernels: 75.6 us -> 69.5 us  [local(): pl.pallas_call(kernel, out_shape=[jax.ShapeDtypeStruct(rows, BF16)] * 3 +...]
    unnamed x16 -> x10, local copies, waits for them, and re-layouts: 9.55 us -> 5.77 us
where the time goes in v2:
time: 76.1 us; the launch traced here: 75.9 us
  Pallas kernels  69.5 us (91%)
  local copies, waits for them, and re-layouts  5.77 us (8%)
    pallas_call x1, Pallas kernels, local(): pl.pallas_call(kernel, out_shape=[jax.ShapeDtypeStruct(rows, BF16)] * 3 +...  69.5 us
    unnamed x10, local copies, waits for them, and re-layouts  5.77 us

profile of v2, /device:TPU:1, one launch (start us, length us, event | category | flops | bytes accessed | tf_op | source)
XLA Modules:
  0.0 75.9 jit_solution(10421221589666935640)
XLA Ops:
  0.6 69.5 %shard_map.111 = (bf16[128,4096]{1,0:T(8,128)(2,1)}, bf16[128,4096]{1,0:T(8,128)(2,1)}, bf16[128,4096]{1,0:T(8,128)(2,1)}, f32[32,16384]{1,0:T(8,128)}) custom-call(bf16[128,4096]{1,0:T(8,128)(2,1)} %q_hbm.1, bf16[128,4096]{1,0:T(8,128)(2,1)} %k_hbm.1, bf16[128,4096]{1,0:T(8,128)(2,1)} %v_hbm.1, bf16[128,4096]{1,0:T(8,128)(2,1)} %g_hbm.1, ...), custom_call_target="tpu_custom_call" | custom-call | flops 5368709120 | bytes 11534336 | tf_op jit(solution)/shard_map/pallas_call | solution.py:284
  70.1 0.0 copy-start.2
  70.1 0.0 copy-start.1
  70.1 2.4 %copy.16 = bf16[128,4096]{1,0:T(8,128)(2,1)} copy(bf16[128,4096]{1,0:T(8,128)(2,1)} %get-tuple-element.16) | data formatting | bytes 2097152
  72.6 0.0 copy-done.2
  72.6 0.0 copy-start
  72.6 1.0 %copy.17 = bf16[128,4096]{1,0:T(8,128)(2,1)} copy(bf16[128,4096]{1,0:T(8,128)(2,1)S(1)} %copy-done.2) | data formatting | bytes 2097152
  73.6 0.0 copy-done.1
  73.6 1.0 %copy.18 = bf16[128,4096]{1,0:T(8,128)(2,1)} copy(bf16[128,4096]{1,0:T(8,128)(2,1)S(1)} %copy-done.1) | data formatting | bytes 2097152
  74.5 0.1 copy-done
  74.6 1.3 %copy.19 = f32[16384,32]{0,1:T(8,128)} copy(f32[16384,32]{0,1:T(8,128)S(1)} %bitcast.2) | data formatting | bytes 4194304
Async XLA Ops:
  70.1 2.5 %copy-start.2 = (bf16[128,4096]{1,0:T(8,128)(2,1)S(1)}, bf16[128,4096]{1,0:T(8,128)(2,1)}, u32[]{:S(2)}) copy-start(bf16[128,4096]{1,0:T(8,128)(2,1)} %get-tuple-element.17) | copy-start | bytes 3145732
  70.1 3.4 %copy-start.1 = (bf16[128,4096]{1,0:T(8,128)(2,1)S(1)}, bf16[128,4096]{1,0:T(8,128)(2,1)}, u32[]{:S(2)}) copy-start(bf16[128,4096]{1,0:T(8,128)(2,1)} %get-tuple-element.18) | copy-start | bytes 3145732
  72.6 2.0 %copy-start = (f32[32,16384]{1,0:T(8,128)S(1)}, f32[32,16384]{1,0:T(8,128)}, u32[]{:S(2)}) copy-start(f32[32,16384]{1,0:T(8,128)} %get-tuple-element.11) | copy-start | bytes 6291460

commit v3 on v2

--- a/solution.py
+++ b/solution.py
@@ -276,15 +276,29 @@
         wait_send(slot)
 
 
+def place(*refs):
+    *pairs, sem = refs
+    half = len(pairs) // 2
+    copies = [
+        pltpu.make_async_copy(src, dst, sem.at[i])
+        for i, (src, dst) in enumerate(zip(pairs[:half], pairs[half:]))
+    ]
+    for copy in copies:
+        copy.start()
+    for copy in copies:
+        copy.wait()
+
+
 def local(queries, keys, values, grad_out, filter_param):
     wide, first, twist = make_tables()
+    operands = (queries, keys, values, grad_out, filter_param.T, wide, first, twist)
     hbm = pl.BlockSpec(memory_space=pltpu.HBM)
     vmem = pl.BlockSpec(memory_space=pltpu.VMEM)
     rows = (N, C)
     out = pl.pallas_call(
         kernel,
-        out_shape=[jax.ShapeDtypeStruct(rows, BF16)] * 3
-        + [jax.ShapeDtypeStruct((W, N * N), F32)],
+        out_shape=[pltpu.VMEM(rows, BF16)] * 3
+        + [pltpu.VMEM((W, N * N), F32)],
         in_specs=[hbm] * 8,
         out_specs=[vmem] * 4,
         scratch_shapes=[
@@ -308,11 +322,18 @@
             pltpu.SemaphoreType.DMA((4,)),
         ],
         compiler_params=pltpu.CompilerParams(
-            collective_id=0, has_side_effects=True, vmem_limit_bytes=62 << 20
+            collective_id=0, has_side_effects=True, vmem_limit_bytes=40 << 20
         ),
         cost_estimate=pl.CostEstimate(flops=5 << 30, bytes_accessed=11 << 20, transcendentals=0),
-    )(queries, keys, values, grad_out, filter_param.T, wide, first, twist)
-    query_grad, key_grad, value_grad, filter_grad = out
+    )(*[pltpu.with_memory_space_constraint(x, pltpu.HBM) for x in operands])
+    query_grad, key_grad, value_grad, filter_grad = pl.pallas_call(
+        place,
+        out_shape=[jax.ShapeDtypeStruct(x.shape, x.dtype) for x in out],
+        in_specs=[pl.BlockSpec(memory_space=pl.ANY)] * 4,
+        out_specs=[hbm] * 4,
+        scratch_shapes=[pltpu.SemaphoreType.DMA((4,))],
+        compiler_params=pltpu.CompilerParams(vmem_limit_bytes=1 << 20),
+    )(*out)
     return query_grad, key_grad, value_grad, filter_grad.T
 
 

time: 76.1 us -> 70.5 us (0.926)
  local copies, waits for them, and re-layouts: 5.77 us -> 0 us
    unnamed x10 -> x0, local copies, waits for them, and re-layouts: 5.77 us -> none
    pallas_call x1 -> x2, Pallas kernels: 69.5 us -> 69.6 us  [the longest x1 67.2 us: local(): pl.pallas_call(kernel, out_shape=[pltpu.VMEM(rows, BF16)] * 3 + [pltpu.VM...]
where the time goes in v3:
time: 70.5 us; the launch traced here: 70.3 us
  Pallas kernels  69.6 us (99%)
    pallas_call x1, Pallas kernels, local(): pl.pallas_call(kernel, out_shape=[pltpu.VMEM(rows, BF16)] * 3 + [pltpu.VM...  67.2 us
    pallas_call x1, Pallas kernels, local(): pl.pallas_call(place, out_shape=[jax.ShapeDtypeStruct(x.shape, x.dtype) f...  2.39 us

profile of v3, /device:TPU:1, one launch (start us, length us, event | category | flops | bytes accessed | tf_op | source)
XLA Modules:
  0.0 70.3 jit_solution(12389918498963192011)
XLA Ops:
  0.6 67.2 %shard_map.111 = (bf16[128,4096]{1,0:T(8,128)(2,1)S(1)}, bf16[128,4096]{1,0:T(8,128)(2,1)S(1)}, bf16[128,4096]{1,0:T(8,128)(2,1)S(1)}, f32[32,16384]{1,0:T(8,128)S(1)}) custom-call(bf16[128,4096]{1,0:T(8,128)(2,1)} %q_hbm.1, bf16[128,4096]{1,0:T(8,128)(2,1)} %k_hbm.1, bf16[128,4096]{1,0:T(8,128)(2,1)} %v_hbm.1, bf16[128,4096]{1,0:T(8,128)(2,1)} %g_hbm.1, ...), custom_call_target="tpu_custom_call" | custom-call | flops 5368709120 | bytes 11534336 | tf_op jit(solution)/shard_map/pallas_call | solution.py:298
  67.9 2.4 %shard_map.112 = (bf16[128,4096]{1,0:T(8,128)(2,1)}, bf16[128,4096]{1,0:T(8,128)(2,1)}, bf16[128,4096]{1,0:T(8,128)(2,1)}, f32[32,16384]{1,0:T(8,128)}) custom-call(bf16[128,4096]{1,0:T(8,128)(2,1)S(1)} %get-tuple-element.12.refs_0_, bf16[128,4096]{1,0:T(8,128)(2,1)S(1)} %get-tuple-element.13.refs_1_, bf16[128,4096]{1,0:T(8,128)(2,1)S(1)} %get-tuple-element.14.refs_2_, ...), custom_call_target="tpu_custom_call" | custom-call | tf_op jit(solution)/shard_map/pallas_call | solution.py:329

commit v4 on v3

--- a/solution.py
+++ b/solution.py
@@ -14,10 +14,11 @@
 BF16 = jnp.bfloat16
 N = 128
 W = 32
+HALF = W // 2
 C = N * W
 GROUP = 4
 UNROLL = 4
-SWAP_UNROLL = 2
+SWAP_UNROLL = 4
 
 
 def make_tables():
@@ -70,18 +71,32 @@
     for load in loads:
         load.start()
 
-    def partner(i):
-        x = (cx + i) % 4
-        y = (cy + i // 4 + i) % 4
-        z = (cz + i // 16 + i // 4 + i) % 4
-        c = (cc + i // 64 + i) % 2
-        return z * 2 + x // 2, y * 4 + (x % 2) * 2 + c
+    xs = [(cx + r) % 4 for r in range(4)]
+    x_dp = [x // 2 for x in xs]
+    x_ctx = [(x % 2) * 2 for x in xs]
+    y_ctx = [((cy + r) % 4) * 4 for r in range(4)]
+    c_ctx = [cc, 1 - cc]
+
+    def partners(visit):
+        @pl.loop(0, 8)
+        def _(m):
+            z_dp = [((cz + m + r) % 4) * 2 for r in range(4)]
+            far = m // 4
+            c_now = [far + (1 - 2 * far) * c for c in c_ctx]
+            for n in range(4):
+                for r in range(4):
+                    d = z_dp[(n + r) % 4] + x_dp[r]
+                    e = y_ctx[(n + r) % 4] + x_ctx[r] + c_now[r % 2]
+                    if n + r == 0:
+                        pl.when(m > 0)(functools.partial(visit, d, e))
+                    else:
+                        visit(d, e)
 
     barrier = pltpu.get_barrier_semaphore()
 
-    @pl.loop(1, N)
-    def _(i):
-        pl.semaphore_signal(barrier, inc=1, device_id=partner(i), device_id_type=MESH)
+    partners(
+        lambda d, e: pl.semaphore_signal(barrier, inc=1, device_id=(d, e), device_id_type=MESH)
+    )
 
     ident = wide.at[512:768]
     swap = wide.at[768:1024]
@@ -95,7 +110,10 @@
                 gated = (left[:, cols].astype(F32) * right[:, cols].astype(F32)).astype(BF16)
                 turned.append(dot_nt(ident[...], gated).astype(BF16))
             for u in range(UNROLL):
-                send[slot, pl.ds(pl.multiple_of(i * (8 * UNROLL) + u * 8, 8), 8)] = turned[u].reshape(8, W, 128)
+                block = turned[u].reshape(8, W, 128)
+                rows = pl.ds(pl.multiple_of(i * (8 * UNROLL) + u * 8, 8), 8)
+                send[slot, rows] = block[:, :HALF]
+                send[slot + 1, rows] = block[:, HALF:]
 
     for load in loads[:3]:
         load.wait()
@@ -103,9 +121,8 @@
     pl.semaphore_wait(barrier, N - 1)
 
     def start_sends(slot):
-        @pl.loop(1, N)
-        def _(i):
-            d, e = partner(i)
+
+        def visit(d, e):
             pltpu.make_async_remote_copy(
                 src_ref=send.at[slot, d * 16 + e],
                 dst_ref=recv.at[slot, me],
@@ -115,68 +132,72 @@
                 device_id_type=MESH,
             ).start()
 
+        partners(visit)
         pltpu.make_async_copy(send.at[slot, me], recv.at[slot, me], own_sem.at[slot]).start()
 
     def wait_recv(slot):
+
         others = recv.at[slot, pl.ds(0, N - 1)]
         pltpu.make_async_copy(others, others, recv_sem.at[slot]).wait()
         pltpu.make_async_copy(send.at[slot, me], recv.at[slot, me], own_sem.at[slot]).wait()
 
     def wait_send(slot):
+
         others = send.at[slot, pl.ds(0, N - 1)]
         pltpu.make_async_copy(others, others, send_sem.at[slot]).wait()
 
     start_sends(0)
+    start_sends(1)
     for load in loads[3:5]:
         load.wait()
-    gate_in(g, q, 1)
-    start_sends(1)
+    gate_in(g, q, 2)
+    start_sends(2)
+    start_sends(3)
     for load in loads[5:]:
         load.wait()
 
     cos, sin = twist.at[0:128], twist.at[128:256]
 
-    def swap_blocks(load_block, store_block):
+    def swap_blocks(half, load_block, store_block):
         @pl.loop(0, 8 // SWAP_UNROLL)
         def _(i):
-            blocks = [(i * SWAP_UNROLL + u, j) for u in range(SWAP_UNROLL) for j in range(2)]
-            found = [dot(swap[...], load_block(*block)) for block in blocks]
+            blocks = [i * SWAP_UNROLL + u for u in range(SWAP_UNROLL)]
+            found = [dot(swap[...], load_block(half, block)) for block in blocks]
             for block, x in zip(blocks, found):
-                store_block(*block, x)
+                store_block(half, block, x)
+
+    def sixteen(i):
+        return pl.ds(pl.multiple_of(i * 16, 16), 16)
+
+    def half_of(half):
+        return pl.ds(half * HALF, HALF)
 
     def recv_block(slot):
-        def load(i, j):
-            rows = recv[slot, pl.ds(pl.multiple_of(i * 16, 16), 16), pl.ds(j * 16, 16), :]
-            return rows.reshape(256, 128)
-
-        return load
-
-    def taps_block(i, j):
+        return lambda half, i: recv[slot + half, sixteen(i)].reshape(256, 128)
+
+    def taps_block(half, i):
         parts = []
         for s in range(16):
             lanes = pl.ds(pl.multiple_of((i * 16 + s) * 128, 128), 128)
-            parts.append(taps[pl.ds(j * 16, 16), lanes])
+            parts.append(taps[half_of(half), lanes])
         return jnp.concatenate(parts, axis=0).astype(BF16)
 
-    def xt_store(i, j, block):
-        rows = pl.ds(pl.multiple_of(i * 16, 16), 16)
-        xt[pl.ds(j * 16, 16), rows, :] = block.astype(BF16).reshape(16, 16, 128)
-
-    def xt_block(i, j):
-        rows = pl.ds(pl.multiple_of(i * 16, 16), 16)
-        return xt[pl.ds(j * 16, 16), rows, :].reshape(256, 128)
+    def xt_store(half, i, block):
+        xt[half_of(half), sixteen(i), :] = block.astype(BF16).reshape(16, 16, 128)
+
+    def xt_block(half, i):
+        return xt[half_of(half), sixteen(i), :].reshape(256, 128)
 
     def send_store(slot):
-        def store(i, j, block):
-            rows = pl.ds(pl.multiple_of(i * 16, 16), 16)
-            send[slot, rows, pl.ds(j * 16, 16), :] = block.astype(BF16).reshape(16, 16, 128)
+        def store(half, i, block):
+            send[slot + half, sixteen(i)] = block.astype(BF16).reshape(16, 16, 128)
 
         return store
 
-    def fg_store(i, j, block):
+    def fg_store(half, i, block):
         for s in range(16):
             lanes = pl.ds(pl.multiple_of((i * 16 + s) * 128, 128), 128)
-            fg_ref[pl.ds(j * 16, 16), lanes] = block[s * 16 : (s + 1) * 16]
+            fg_ref[half_of(half), lanes] = block[s * 16 : (s + 1) * 16]
 
     def forward(ws):
         outer = [dot(first[...], xt[w]) for w in ws]
@@ -209,21 +230,14 @@
         xr, xi, yr, yi = x[:, :128], x[:, 128:], y[:, :128], y[:, 128:]
         return jnp.concatenate([xr * yr + xi * yi, xr * yi - xi * yr], axis=1).astype(BF16)
 
-    def groups(body):
-        @pl.loop(0, W // GROUP)
+    def groups(half, body):
+        @pl.loop(half * HALF // GROUP, (half + 1) * HALF // GROUP)
         def _(i):
             body([i * GROUP + j for j in range(GROUP)])
-
-    swap_blocks(taps_block, xt_store)
 
     def taps_step(ws):
         for w, x in zip(ws, forward(ws)):
             spec_h[w] = x.astype(BF16)
-
-    groups(taps_step)
-
-    wait_recv(0)
-    swap_blocks(recv_block(0), xt_store)
 
     def gated_step(ws):
         found = forward(ws)
@@ -231,32 +245,33 @@
             spec_g[w] = x.astype(BF16)
         backward(ws, [product(x, spec_h[w].astype(F32)) for w, x in zip(ws, found)])
 
-    groups(gated_step)
-    swap_blocks(xt_block, send_store(2))
-    start_sends(2)
-
-    wait_recv(1)
-    swap_blocks(recv_block(1), xt_store)
-
     def grad_step(ws):
         found = forward(ws)
         for w, x in zip(ws, found):
             spec_q[w] = x.astype(BF16)
         backward(ws, [conj_product(spec_h[w].astype(F32), x) for w, x in zip(ws, found)])
 
-    groups(grad_step)
-    swap_blocks(xt_block, send_store(3))
-    start_sends(3)
-
     def filter_step(ws):
         backward(ws, [conj_product(spec_g[w].astype(F32), spec_q[w].astype(F32)) for w in ws])
 
-    groups(filter_step)
-    swap_blocks(xt_block, fg_store)
+    for half in range(2):
+        swap_blocks(half, taps_block, xt_store)
+        groups(half, taps_step)
+    for slot, step in ((0, gated_step), (2, grad_step)):
+        for half in range(2):
+            wait_recv(slot + half)
+            swap_blocks(half, recv_block(slot), xt_store)
+            groups(half, step)
+            swap_blocks(half, xt_block, send_store(slot + 4))
+            start_sends(slot + 4 + half)
+    for half in range(2):
+        groups(half, filter_step)
+        swap_blocks(half, xt_block, fg_store)
 
     def turned(slot, i):
-        rows = recv[slot, pl.ds(pl.multiple_of(i * 8, 8), 8)].reshape(256, 128)
-        return dot_nt(wide[512:640, 0:128], rows)
+        rows = pl.ds(pl.multiple_of(i * 8, 8), 8)
+        both = jnp.concatenate([recv[slot, rows], recv[slot + 1, rows]], axis=1)
+        return dot_nt(wide[512:640, 0:128], both.reshape(256, 128))
 
     def gate_out(slot, pairs):
         @pl.loop(0, C // 256 // UNROLL)
@@ -267,12 +282,13 @@
                 for out_ref, gate in pairs:
                     out_ref[:, cols] = (gate[:, cols].astype(F32) * found[u]).astype(BF16)
 
-    wait_recv(2)
-    gate_out(2, [(qg_ref, g)])
-    wait_recv(3)
-    gate_out(3, [(kg_ref, v), (vg_ref, k)])
-
-    for slot in range(4):
+    wait_recv(4)
+    wait_recv(5)
+    gate_out(4, [(qg_ref, g)])
+    wait_recv(6)
+    wait_recv(7)
+    gate_out(6, [(kg_ref, v), (vg_ref, k)])
+    for slot in range(8):
         wait_send(slot)
 
 
@@ -310,16 +326,16 @@
             pltpu.VMEM(wide.shape, BF16),
             pltpu.VMEM(first.shape, BF16),
             pltpu.VMEM(twist.shape, F32),
-            pltpu.VMEM((4, N, W, 128), BF16),
-            pltpu.VMEM((4, N, W, 128), BF16),
+            pltpu.VMEM((8, N, HALF, 128), BF16),
+            pltpu.VMEM((8, N, HALF, 128), BF16),
             pltpu.VMEM((W, 128, 128), BF16),
             pltpu.VMEM((W, 128, 256), BF16),
             pltpu.VMEM((W, 128, 256), BF16),
             pltpu.VMEM((W, 128, 256), BF16),
             pltpu.SemaphoreType.DMA((8,)),
-            pltpu.SemaphoreType.DMA((4,)),
-            pltpu.SemaphoreType.DMA((4,)),
-            pltpu.SemaphoreType.DMA((4,)),
+            pltpu.SemaphoreType.DMA((8,)),
+            pltpu.SemaphoreType.DMA((8,)),
+            pltpu.SemaphoreType.DMA((8,)),
         ],
         compiler_params=pltpu.CompilerParams(
             collective_id=0, has_side_effects=True, vmem_limit_bytes=40 << 20

time: 70.5 us -> 63.7 us (0.904)
  Pallas kernels: 69.6 us -> 62.9 us
    pallas_call x1, Pallas kernels: 67.2 us -> 60.5 us  [local(): pl.pallas_call(kernel, out_shape=[pltpu.VMEM(rows, BF16)] * 3 + [pltpu.VM...]
where the time goes in v4:
time: 63.7 us; the launch traced here: 63.6 us
  Pallas kernels  62.9 us (99%)
  between operations  0.64 us (1%)
    pallas_call x1, Pallas kernels, local(): pl.pallas_call(kernel, out_shape=[pltpu.VMEM(rows, BF16)] * 3 + [pltpu.VM...  60.5 us
    pallas_call x1, Pallas kernels, local(): pl.pallas_call(place, out_shape=[jax.ShapeDtypeStruct(x.shape, x.dtype) f...  2.39 us

profile of v4, /device:TPU:1, one launch (start us, length us, event | category | flops | bytes accessed | tf_op | source)
XLA Modules:
  0.0 63.6 jit_solution(15108658984951912712)
XLA Ops:
  0.6 60.5 %shard_map.111 = (bf16[128,4096]{1,0:T(8,128)(2,1)S(1)}, bf16[128,4096]{1,0:T(8,128)(2,1)S(1)}, bf16[128,4096]{1,0:T(8,128)(2,1)S(1)}, f32[32,16384]{1,0:T(8,128)S(1)}) custom-call(bf16[128,4096]{1,0:T(8,128)(2,1)} %q_hbm.1, bf16[128,4096]{1,0:T(8,128)(2,1)} %k_hbm.1, bf16[128,4096]{1,0:T(8,128)(2,1)} %v_hbm.1, bf16[128,4096]{1,0:T(8,128)(2,1)} %g_hbm.1, ...), custom_call_target="tpu_custom_call" | custom-call | flops 5368709120 | bytes 11534336 | tf_op jit(solution)/shard_map/pallas_call | solution.py:314
  61.2 2.4 %shard_map.112 = (bf16[128,4096]{1,0:T(8,128)(2,1)}, bf16[128,4096]{1,0:T(8,128)(2,1)}, bf16[128,4096]{1,0:T(8,128)(2,1)}, f32[32,16384]{1,0:T(8,128)}) custom-call(bf16[128,4096]{1,0:T(8,128)(2,1)S(1)} %get-tuple-element.12.refs_0_, bf16[128,4096]{1,0:T(8,128)(2,1)S(1)} %get-tuple-element.13.refs_1_, bf16[128,4096]{1,0:T(8,128)(2,1)S(1)} %get-tuple-element.14.refs_2_, ...), custom_call_target="tpu_custom_call" | custom-call | tf_op jit(solution)/shard_map/pallas_call | solution.py:345

commit v5 on v4

--- a/solution.py
+++ b/solution.py
@@ -50,10 +50,22 @@
     return lax.dot_general(x, y, (((1,), (1,)), ((), ())), preferred_element_type=F32)
 
 
+def gate_out(i, unit, low, high, pairs):
+    found = []
+    for u in range(UNROLL):
+        rows = pl.ds(pl.multiple_of((i * UNROLL + u) * 8, 8), 8)
+        both = jnp.concatenate([low[rows], high[rows]], axis=1)
+        found.append(dot_nt(unit, both.reshape(256, 128)))
+    for u in range(UNROLL):
+        cols = pl.ds(pl.multiple_of((i * UNROLL + u) * 256, 256), 256)
+        for out_ref, gate in pairs:
+            out_ref[:, cols] = (gate[:, cols].astype(F32) * found[u]).astype(BF16)
+
+
 def kernel(
     q_hbm, k_hbm, v_hbm, g_hbm, taps_hbm, wide_hbm, first_hbm, twist_hbm,
-    qg_ref, kg_ref, vg_ref, fg_ref,
-    q, k, v, g, taps, wide, first, twist,
+    qg_ref, fg_ref, back, k, v,
+    q, g, taps, wide, first, twist,
     send, recv, xt, spec_h, spec_g, spec_q,
     load_sem, send_sem, recv_sem, own_sem,
 ):
@@ -68,7 +80,7 @@
              (first_hbm, first), (twist_hbm, twist), (taps_hbm, taps)]
         )
     ]
-    for load in loads:
+    for load in loads[:3]:
         load.start()
 
     xs = [(cx + r) % 4 for r in range(4)]
@@ -97,6 +109,8 @@
     partners(
         lambda d, e: pl.semaphore_signal(barrier, inc=1, device_id=(d, e), device_id_type=MESH)
     )
+    for load in loads[3:]:
+        load.start()
 
     ident = wide.at[512:768]
     swap = wide.at[768:1024]
@@ -120,12 +134,15 @@
     gate_in(k, v, 0)
     pl.semaphore_wait(barrier, N - 1)
 
+    def landing(slot):
+        return recv.at[slot] if slot < 6 else back.at[slot - 6]
+
     def start_sends(slot):
 
         def visit(d, e):
             pltpu.make_async_remote_copy(
                 src_ref=send.at[slot, d * 16 + e],
-                dst_ref=recv.at[slot, me],
+                dst_ref=landing(slot).at[me],
                 send_sem=send_sem.at[slot],
                 recv_sem=recv_sem.at[slot],
                 device_id=(d, e),
@@ -133,13 +150,13 @@
             ).start()
 
         partners(visit)
-        pltpu.make_async_copy(send.at[slot, me], recv.at[slot, me], own_sem.at[slot]).start()
+        pltpu.make_async_copy(send.at[slot, me], landing(slot).at[me], own_sem.at[slot]).start()
 
     def wait_recv(slot):
 
-        others = recv.at[slot, pl.ds(0, N - 1)]
+        others = landing(slot).at[pl.ds(0, N - 1)]
         pltpu.make_async_copy(others, others, recv_sem.at[slot]).wait()
-        pltpu.make_async_copy(send.at[slot, me], recv.at[slot, me], own_sem.at[slot]).wait()
+        pltpu.make_async_copy(send.at[slot, me], landing(slot).at[me], own_sem.at[slot]).wait()
 
     def wait_send(slot):
 
@@ -268,39 +285,38 @@
         groups(half, filter_step)
         swap_blocks(half, xt_block, fg_store)
 
-    def turned(slot, i):
-        rows = pl.ds(pl.multiple_of(i * 8, 8), 8)
-        both = jnp.concatenate([recv[slot, rows], recv[slot + 1, rows]], axis=1)
-        return dot_nt(wide[512:640, 0:128], both.reshape(256, 128))
-
-    def gate_out(slot, pairs):
-        @pl.loop(0, C // 256 // UNROLL)
-        def _(i):
-            found = [turned(slot, i * UNROLL + u) for u in range(UNROLL)]
-            for u in range(UNROLL):
-                cols = pl.ds(pl.multiple_of(i * (256 * UNROLL) + u * 256, 256), 256)
-                for out_ref, gate in pairs:
-                    out_ref[:, cols] = (gate[:, cols].astype(F32) * found[u]).astype(BF16)
-
     wait_recv(4)
     wait_recv(5)
-    gate_out(4, [(qg_ref, g)])
+
+    @pl.loop(0, C // 256 // UNROLL)
+    def _(i):
+        gate_out(i, wide[512:640, 0:128], recv.at[4], recv.at[5], [(qg_ref, g)])
+
     wait_recv(6)
     wait_recv(7)
-    gate_out(6, [(kg_ref, v), (vg_ref, k)])
     for slot in range(8):
         wait_send(slot)
 
 
-def place(*refs):
-    *pairs, sem = refs
-    half = len(pairs) // 2
+def finish(
+    qg, fg, back, k, v, qg_hbm, fg_hbm, kg_hbm, vg_hbm, kg, vg, sem
+):
     copies = [
-        pltpu.make_async_copy(src, dst, sem.at[i])
-        for i, (src, dst) in enumerate(zip(pairs[:half], pairs[half:]))
+        pltpu.make_async_copy(fg, fg_hbm, sem.at[0]),
+        pltpu.make_async_copy(qg, qg_hbm, sem.at[1]),
     ]
     for copy in copies:
         copy.start()
+    rows = lax.broadcasted_iota(jnp.int32, (128, 128), 0)
+    unit = (rows == lax.broadcasted_iota(jnp.int32, (128, 128), 1)).astype(F32).astype(BF16)
+    steps = C // 256 // UNROLL
+    for i in range(steps):
+        gate_out(i, unit, back.at[0], back.at[1], [(kg, v), (vg, k)])
+        cols = pl.ds(i * 256 * UNROLL, 256 * UNROLL)
+        for j, (src, dst) in enumerate([(kg, kg_hbm), (vg, vg_hbm)]):
+            copy = pltpu.make_async_copy(src.at[:, cols], dst.at[:, cols], sem.at[2 + 2 * i + j])
+            copy.start()
+            copies.append(copy)
     for copy in copies:
         copy.wait()
 
@@ -313,13 +329,16 @@
     rows = (N, C)
     out = pl.pallas_call(
         kernel,
-        out_shape=[pltpu.VMEM(rows, BF16)] * 3
-        + [pltpu.VMEM((W, N * N), F32)],
+        out_shape=[
+            pltpu.VMEM(rows, BF16),
+            pltpu.VMEM((W, N * N), F32),
+            pltpu.VMEM((2, N, HALF, 128), BF16),
+            pltpu.VMEM(rows, BF16),
+            pltpu.VMEM(rows, BF16),
+        ],
         in_specs=[hbm] * 8,
-        out_specs=[vmem] * 4,
+        out_specs=[vmem] * 5,
         scratch_shapes=[
-            pltpu.VMEM(rows, BF16),
-            pltpu.VMEM(rows, BF16),
             pltpu.VMEM(rows, BF16),
             pltpu.VMEM(rows, BF16),
             pltpu.VMEM((W, N * N), F32),
@@ -327,7 +346,7 @@
             pltpu.VMEM(first.shape, BF16),
             pltpu.VMEM(twist.shape, F32),
             pltpu.VMEM((8, N, HALF, 128), BF16),
-            pltpu.VMEM((8, N, HALF, 128), BF16),
+            pltpu.VMEM((6, N, HALF, 128), BF16),
             pltpu.VMEM((W, 128, 128), BF16),
             pltpu.VMEM((W, 128, 256), BF16),
             pltpu.VMEM((W, 128, 256), BF16),
@@ -342,13 +361,22 @@
         ),
         cost_estimate=pl.CostEstimate(flops=5 << 30, bytes_accessed=11 << 20, transcendentals=0),
     )(*[pltpu.with_memory_space_constraint(x, pltpu.HBM) for x in operands])
-    query_grad, key_grad, value_grad, filter_grad = pl.pallas_call(
-        place,
-        out_shape=[jax.ShapeDtypeStruct(x.shape, x.dtype) for x in out],
-        in_specs=[pl.BlockSpec(memory_space=pl.ANY)] * 4,
+    query_grad, filter_grad, key_grad, value_grad = pl.pallas_call(
+        finish,
+        out_shape=[
+            jax.ShapeDtypeStruct(rows, BF16),
+            jax.ShapeDtypeStruct((W, N * N), F32),
+            jax.ShapeDtypeStruct(rows, BF16),
+            jax.ShapeDtypeStruct(rows, BF16),
+        ],
+        in_specs=[pl.BlockSpec(memory_space=pl.ANY)] * 2 + [vmem] * 3,
         out_specs=[hbm] * 4,
-        scratch_shapes=[pltpu.SemaphoreType.DMA((4,))],
-        compiler_params=pltpu.CompilerParams(vmem_limit_bytes=1 << 20),
+        scratch_shapes=[
+            pltpu.VMEM(rows, BF16),
+            pltpu.VMEM(rows, BF16),
+            pltpu.SemaphoreType.DMA((2 + 2 * (C // 256 // UNROLL),)),
+        ],
+        compiler_params=pltpu.CompilerParams(vmem_limit_bytes=8 << 20),
     )(*out)
     return query_grad, key_grad, value_grad, filter_grad.T
 

time: 63.7 us -> 62.6 us (0.983)
  Pallas kernels: 62.9 us -> 61.9 us
    pallas_call x2, Pallas kernels: 62.9 us -> 61.9 us  [the longest x1 59.5 us: local(): pl.pallas_call(kernel, out_shape=[pltpu.VMEM(rows, BF16), pltpu.VMEM((W,...]
where the time goes in v5:
time: 62.6 us; the launch traced here: 62.5 us
  Pallas kernels  61.9 us (99%)
  between operations  0.64 us (1%)
    pallas_call x1, Pallas kernels, local(): pl.pallas_call(kernel, out_shape=[pltpu.VMEM(rows, BF16), pltpu.VMEM((W,...  59.5 us
    pallas_call x1, Pallas kernels, local(): pl.pallas_call(finish, out_shape=[jax.ShapeDtypeStruct(rows, BF16), jax.S...  2.41 us

profile of v5, /device:TPU:1, one launch (start us, length us, event | category | flops | bytes accessed | tf_op | source)
XLA Modules:
  0.0 62.5 jit_solution(2068809804671582239)
XLA Ops:
  0.6 59.5 %shard_map.111 = (bf16[128,4096]{1,0:T(8,128)(2,1)S(1)}, f32[32,16384]{1,0:T(8,128)S(1)}, bf16[2,128,16,128]{3,2,1,0:T(8,128)(2,1)S(1)}, bf16[128,4096]{1,0:T(8,128)(2,1)S(1)}, bf16[128,4096]{1,0:T(8,128)(2,1)S(1)}) custom-call(bf16[128,4096]{1,0:T(8,128)(2,1)} %q_hbm.1, bf16[128,4096]{1,0:T(8,128)(2,1)} %k_hbm.1, bf16[128,4096]{1,0:T(8,128)(2,1)} %v_hbm.1, ...), custom_call_target="tpu_custom_call" | custom-call | flops 5368709120 | bytes 11534336 | tf_op jit(solution)/shard_map/pallas_call | solution.py:330
  60.1 2.4 %shard_map.112 = (bf16[128,4096]{1,0:T(8,128)(2,1)}, f32[32,16384]{1,0:T(8,128)}, bf16[128,4096]{1,0:T(8,128)(2,1)}, bf16[128,4096]{1,0:T(8,128)(2,1)}) custom-call(bf16[128,4096]{1,0:T(8,128)(2,1)S(1)} %get-tuple-element.13.qg, f32[32,16384]{1,0:T(8,128)S(1)} %get-tuple-element.14.fg, bf16[2,128,16,128]{3,2,1,0:T(8,128)(2,1)S(1)} %get-tuple-element.15.back, ...), custom_call_target="tpu_custom_call" | custom-call | tf_op jit(solution)/shard_map/pallas_call | solution.py:364

commit v6 on v5

--- a/solution.py
+++ b/solution.py
@@ -34,6 +34,8 @@
     index = np.arange(256)
     swap = np.zeros((256, 256))
     swap[index, (index % 16) * 16 + index // 16] = 1.0
+    first_high = first.astype(BF16).astype(np.float64)
+    first = np.concatenate([first_high, first - first_high], axis=1)
     wide = np.concatenate([second, second.T, np.eye(256), swap, last], axis=0)
     return (
         jnp.asarray(wide.astype(np.float32), BF16),
@@ -66,7 +68,7 @@
     q_hbm, k_hbm, v_hbm, g_hbm, taps_hbm, wide_hbm, first_hbm, twist_hbm,
     qg_ref, fg_ref, back, k, v,
     q, g, taps, wide, first, twist,
-    send, recv, xt, spec_h, spec_g, spec_q,
+    send, recv, xt, xt_rest, spec_h, spec_g, spec_q,
     load_sem, send_sem, recv_sem, own_sem,
 ):
     dp, ctx = lax.axis_index("dp"), lax.axis_index("ctx")
@@ -211,13 +213,17 @@
 
         return store
 
+    def rest_block(half, i):
+        return xt_rest[half_of(half), sixteen(i), :].reshape(256, 128)
+
     def fg_store(half, i, block):
+        block = block + dot(swap[...], rest_block(half, i))
         for s in range(16):
             lanes = pl.ds(pl.multiple_of((i * 16 + s) * 128, 128), 128)
             fg_ref[half_of(half), lanes] = block[s * 16 : (s + 1) * 16]
 
     def forward(ws):
-        outer = [dot(first[...], xt[w]) for w in ws]
+        outer = [dot(first[...], jnp.concatenate([xt[w], xt[w]], axis=0)) for w in ws]
         twisted = []
         for x in outer:
             re, im = x[:128], x[128:]
@@ -227,7 +233,7 @@
             )
         return [dot(x, wide[0:256]) for x in twisted]
 
-    def backward(ws, products):
+    def backward(ws, products, keep_rest=False):
         inner = [dot(x, wide[256:512]) for x in products]
         twisted = []
         for x in inner:
@@ -237,7 +243,10 @@
                 jnp.concatenate([re * c - im * s, re * s + im * c], axis=0).astype(BF16)
             )
         for w, x in zip(ws, twisted):
-            xt[w] = dot(wide[1024:1152], x).astype(BF16)
+            y = dot(wide[1024:1152], x)
+            xt[w] = y.astype(BF16)
+            if keep_rest:
+                xt_rest[w] = (y - y.astype(BF16).astype(F32)).astype(BF16)
 
     def product(x, y):
         xr, xi, yr, yi = x[:, :128], x[:, 128:], y[:, :128], y[:, 128:]
@@ -254,22 +263,22 @@
 
     def taps_step(ws):
         for w, x in zip(ws, forward(ws)):
-            spec_h[w] = x.astype(BF16)
+            spec_h[w] = x
 
     def gated_step(ws):
         found = forward(ws)
         for w, x in zip(ws, found):
-            spec_g[w] = x.astype(BF16)
-        backward(ws, [product(x, spec_h[w].astype(F32)) for w, x in zip(ws, found)])
+            spec_g[w] = x
+        backward(ws, [product(x, spec_h[w]) for w, x in zip(ws, found)])
 
     def grad_step(ws):
         found = forward(ws)
         for w, x in zip(ws, found):
-            spec_q[w] = x.astype(BF16)
-        backward(ws, [conj_product(spec_h[w].astype(F32), x) for w, x in zip(ws, found)])
+            spec_q[w] = x
+        backward(ws, [conj_product(spec_h[w], x) for w, x in zip(ws, found)])
 
     def filter_step(ws):
-        backward(ws, [conj_product(spec_g[w].astype(F32), spec_q[w].astype(F32)) for w in ws])
+        backward(ws, [conj_product(spec_g[w], spec_q[w]) for w in ws], keep_rest=True)
 
     for half in range(2):
         swap_blocks(half, taps_block, xt_store)
@@ -348,9 +357,10 @@
             pltpu.VMEM((8, N, HALF, 128), BF16),
             pltpu.VMEM((6, N, HALF, 128), BF16),
             pltpu.VMEM((W, 128, 128), BF16),
-            pltpu.VMEM((W, 128, 256), BF16),
-            pltpu.VMEM((W, 128, 256), BF16),
-            pltpu.VMEM((W, 128, 256), BF16),
+            pltpu.VMEM((W, 128, 128), BF16),
+            pltpu.VMEM((W, 128, 256), F32),
+            pltpu.VMEM((W, 128, 256), F32),
+            pltpu.VMEM((W, 128, 256), F32),
             pltpu.SemaphoreType.DMA((8,)),
             pltpu.SemaphoreType.DMA((8,)),
             pltpu.SemaphoreType.DMA((8,)),

time: 62.6 us -> 62.6 us (level)
  no operation moved by 1% of the time
where the time goes in v6:
time: 62.6 us; the launch traced here: 62.5 us
  Pallas kernels  61.9 us (99%)
  between operations  0.64 us (1%)
    pallas_call x1, Pallas kernels, local(): pl.pallas_call(kernel, out_shape=[pltpu.VMEM(rows, BF16), pltpu.VMEM((W,...  59.5 us
    pallas_call x1, Pallas kernels, local(): pl.pallas_call(finish, out_shape=[jax.ShapeDtypeStruct(rows, BF16), jax.S...  2.41 us

profile of v6, /device:TPU:1, one launch (start us, length us, event | category | flops | bytes accessed | tf_op | source)
XLA Modules:
  0.0 62.5 jit_solution(6590176764550874721)
XLA Ops:
  0.6 59.5 %shard_map.111 = (bf16[128,4096]{1,0:T(8,128)(2,1)S(1)}, f32[32,16384]{1,0:T(8,128)S(1)}, bf16[2,128,16,128]{3,2,1,0:T(8,128)(2,1)S(1)}, bf16[128,4096]{1,0:T(8,128)(2,1)S(1)}, bf16[128,4096]{1,0:T(8,128)(2,1)S(1)}) custom-call(bf16[128,4096]{1,0:T(8,128)(2,1)} %q_hbm.1, bf16[128,4096]{1,0:T(8,128)(2,1)} %k_hbm.1, bf16[128,4096]{1,0:T(8,128)(2,1)} %v_hbm.1, ...), custom_call_target="tpu_custom_call" | custom-call | flops 5368709120 | bytes 11534336 | tf_op jit(solution)/shard_map/pallas_call | solution.py:339
  60.1 2.4 %shard_map.112 = (bf16[128,4096]{1,0:T(8,128)(2,1)}, f32[32,16384]{1,0:T(8,128)}, bf16[128,4096]{1,0:T(8,128)(2,1)}, bf16[128,4096]{1,0:T(8,128)(2,1)}) custom-call(bf16[128,4096]{1,0:T(8,128)(2,1)S(1)} %get-tuple-element.13.qg, f32[32,16384]{1,0:T(8,128)S(1)} %get-tuple-element.14.fg, bf16[2,128,16,128]{3,2,1,0:T(8,128)(2,1)S(1)} %get-tuple-element.15.back, ...), custom_call_target="tpu_custom_call" | custom-call | tf_op jit(solution)/shard_map/pallas_call | solution.py:374

commit v7 on v6

--- a/solution.py
+++ b/solution.py
@@ -52,6 +52,12 @@
     return lax.dot_general(x, y, (((1,), (1,)), ((), ())), preferred_element_type=F32)
 
 
+def unit_matrix(size):
+    rows = lax.broadcasted_iota(jnp.int32, (size, size), 0)
+    cols = lax.broadcasted_iota(jnp.int32, (size, size), 1)
+    return (rows == cols).astype(F32).astype(BF16)
+
+
 def gate_out(i, unit, low, high, pairs):
     found = []
     for u in range(UNROLL):
@@ -78,11 +84,11 @@
     loads = [
         pltpu.make_async_copy(src, dst, load_sem.at[i])
         for i, (src, dst) in enumerate(
-            [(wide_hbm, wide), (k_hbm, k), (v_hbm, v), (q_hbm, q), (g_hbm, g),
+            [(k_hbm, k), (v_hbm, v), (wide_hbm, wide), (q_hbm, q), (g_hbm, g),
              (first_hbm, first), (twist_hbm, twist), (taps_hbm, taps)]
         )
     ]
-    for load in loads[:3]:
+    for load in loads[:2]:
         load.start()
 
     xs = [(cx + r) % 4 for r in range(4)]
@@ -111,10 +117,10 @@
     partners(
         lambda d, e: pl.semaphore_signal(barrier, inc=1, device_id=(d, e), device_id_type=MESH)
     )
-    for load in loads[3:]:
+    for load in loads[2:]:
         load.start()
 
-    ident = wide.at[512:768]
+    ident = unit_matrix(256)
     swap = wide.at[768:1024]
 
     def gate_in(left, right, slot):
@@ -124,14 +130,14 @@
             for u in range(UNROLL):
                 cols = pl.ds(pl.multiple_of(i * (256 * UNROLL) + u * 256, 256), 256)
                 gated = (left[:, cols].astype(F32) * right[:, cols].astype(F32)).astype(BF16)
-                turned.append(dot_nt(ident[...], gated).astype(BF16))
+                turned.append(dot_nt(ident, gated).astype(BF16))
             for u in range(UNROLL):
                 block = turned[u].reshape(8, W, 128)
                 rows = pl.ds(pl.multiple_of(i * (8 * UNROLL) + u * 8, 8), 8)
                 send[slot, rows] = block[:, :HALF]
                 send[slot + 1, rows] = block[:, HALF:]
 
-    for load in loads[:3]:
+    for load in loads[:2]:
         load.wait()
     gate_in(k, v, 0)
     pl.semaphore_wait(barrier, N - 1)
@@ -172,7 +178,7 @@
     gate_in(g, q, 2)
     start_sends(2)
     start_sends(3)
-    for load in loads[5:]:
+    for load in loads[5:] + loads[2:3]:
         load.wait()
 
     cos, sin = twist.at[0:128], twist.at[128:256]
@@ -316,8 +322,7 @@
     ]
     for copy in copies:
         copy.start()
-    rows = lax.broadcasted_iota(jnp.int32, (128, 128), 0)
-    unit = (rows == lax.broadcasted_iota(jnp.int32, (128, 128), 1)).astype(F32).astype(BF16)
+    unit = unit_matrix(128)
     steps = C // 256 // UNROLL
     for i in range(steps):
         gate_out(i, unit, back.at[0], back.at[1], [(kg, v), (vg, k)])

time: 62.6 us -> 62.6 us (level)
  no operation moved by 1% of the time
where the time goes in v7:
time: 62.6 us; the launch traced here: 62.5 us
  Pallas kernels  61.9 us (99%)
  between operations  0.64 us (1%)
    pallas_call x1, Pallas kernels, local(): pl.pallas_call(kernel, out_shape=[pltpu.VMEM(rows, BF16), pltpu.VMEM((W,...  59.5 us
    pallas_call x1, Pallas kernels, local(): pl.pallas_call(finish, out_shape=[jax.ShapeDtypeStruct(rows, BF16), jax.S...  2.41 us

profile of v7, /device:TPU:1, one launch (start us, length us, event | category | flops | bytes accessed | tf_op | source)
XLA Modules:
  0.0 62.5 jit_solution(15789823729780014909)
XLA Ops:
  0.6 59.5 %shard_map.111 = (bf16[128,4096]{1,0:T(8,128)(2,1)S(1)}, f32[32,16384]{1,0:T(8,128)S(1)}, bf16[2,128,16,128]{3,2,1,0:T(8,128)(2,1)S(1)}, bf16[128,4096]{1,0:T(8,128)(2,1)S(1)}, bf16[128,4096]{1,0:T(8,128)(2,1)S(1)}) custom-call(bf16[128,4096]{1,0:T(8,128)(2,1)} %q_hbm.1, bf16[128,4096]{1,0:T(8,128)(2,1)} %k_hbm.1, bf16[128,4096]{1,0:T(8,128)(2,1)} %v_hbm.1, ...), custom_call_target="tpu_custom_call" | custom-call | flops 5368709120 | bytes 11534336 | tf_op jit(solution)/shard_map/pallas_call | solution.py:344
  60.1 2.4 %shard_map.112 = (bf16[128,4096]{1,0:T(8,128)(2,1)}, f32[32,16384]{1,0:T(8,128)}, bf16[128,4096]{1,0:T(8,128)(2,1)}, bf16[128,4096]{1,0:T(8,128)(2,1)}) custom-call(bf16[128,4096]{1,0:T(8,128)(2,1)S(1)} %get-tuple-element.13.qg, f32[32,16384]{1,0:T(8,128)S(1)} %get-tuple-element.14.fg, bf16[2,128,16,128]{3,2,1,0:T(8,128)(2,1)S(1)} %get-tuple-element.15.back, ...), custom_call_target="tpu_custom_call" | custom-call | tf_op jit(solution)/shard_map/pallas_call | solution.py:379
